TPU v7x, 128 devices: a whole 4x4x4 slice. The times are simulated.
128 devices in a mesh: row: 8 (over z, x_hi), col: 16 (over x_lo, y, core).
Axes of the slice: x: 4 (x_hi: 2, x_lo: 2; x = x_hi * 2 + x_lo), y: 4, z: 4, core: 2. Of those that a mesh axis runs over, the one named last changes fastest.
Arguments:
- tokens: bfloat16 [4096, 3584], P(('row', 'col')), may hold values from -24 to 24
- cotangent: bfloat16 [4096, 3584], P(('row', 'col')), may hold values from -6 to 6
- router: bfloat16 [3584, 128], replicated, may hold values from -0.09375 to 0.09375
- picks: int32 [4096, 8], P(('row', 'col')), may hold values from 0 to 127, all different within a row; in each aligned block of 32 rows (0 to 31, 32 to 63, ...) at most 3 rows name the same one
- language: int32 [4096], P(('row', 'col')), may hold values from 0 to 7
- teacher: float32 [8, 128], replicated, may hold values from 0.02 to 0.98
- w_gate: bfloat16 [128, 3584, 1024], P(('row', 'col')), may hold values from -0.09375 to 0.09375
- w_up: bfloat16 [128, 3584, 1024], P(('row', 'col')), may hold values from -0.09375 to 0.09375
- w_down: bfloat16 [128, 1024, 3584], P(('row', 'col')), may hold values from -0.1875 to 0.1875
Outputs:
- token_grad: bfloat16 [4096, 3584], P(('row', 'col'))
- router_grad: float32 [3584, 128], P(('row', 'col'))
Inputs may be any that keep to these rules, and one draw needn't show every extreme that they name: `picks`: each token names 8 different experts. Within the rows of one device (aligned blocks of 32 tokens) no expert is named by more than 3 tokens, a bound that some block reaches.
All inputs are finite; a program needn't handle non-finite values.
Results may differ from a plain program's by a relative error of at most 0.007.
Values may be sent and summed in bfloat16 or wider, within the bound.
A program may use at most 128 MiB of HBM per device.

v0:
```python
import math

import jax
import jax.numpy as jnp
from jax import lax
from jax.sharding import PartitionSpec as P

ROUTE_SCALE = 2.5


def silu_parts(values):
    sigma = jax.nn.sigmoid(values)
    return (values * sigma, sigma * (1.0 + values * (1.0 - sigma)))


def slots_of(block_picks, expert_count):
    flat = block_picks.reshape(-1)
    one_hot = (flat[:, None] == jnp.arange(expert_count, dtype=jnp.int32)[None, :]).astype(
        jnp.int32
    )
    before = jnp.cumsum(one_hot, axis=0) - one_hot
    return jnp.sum(before * one_hot, axis=1)


def expert_backward(rows_in, rows_cot, gate_w, up_w, down_w):
    gate_pre = jnp.dot(rows_in, gate_w, preferred_element_type=jnp.float32)
    up_pre = jnp.dot(rows_in, up_w, preferred_element_type=jnp.float32)
    back = jnp.dot(rows_cot, down_w.T, preferred_element_type=jnp.float32)
    active, slope = silu_parts(gate_pre)
    pick_grad = jnp.sum(back * active * up_pre, axis=1).astype(jnp.bfloat16)
    gate_grad = (back * up_pre * slope).astype(jnp.bfloat16)
    up_grad = (back * active).astype(jnp.bfloat16)
    expert_grad = (
        jnp.dot(gate_grad, gate_w.T, preferred_element_type=jnp.float32)
        + jnp.dot(up_grad, up_w.T, preferred_element_type=jnp.float32)
    ).astype(jnp.bfloat16)
    return (expert_grad, pick_grad)


def column_term(tokens, dlogit):
    return lax.dot_general(
        tokens, dlogit, (((0,), (0,)), ((), ())), preferred_element_type=jnp.float32
    )


def local(tokens, cotangent, router, picks, language, teacher, w_gate, w_up, w_down):
    tok_dev, model_width = tokens.shape
    top_count = picks.shape[1]
    expert_count = router.shape[1]
    lang_count = teacher.shape[0]
    capacity = 3 * tok_dev * top_count // (2 * expert_count)
    devices = lax.axis_size(("row", "col"))
    total_tokens = tok_dev * devices
    logits = jnp.dot(tokens, router, preferred_element_type=jnp.float32)
    scores = jax.nn.sigmoid(logits)
    picked = jnp.take_along_axis(scores, picks, axis=1)
    route_w = ROUTE_SCALE * picked / jnp.sum(picked, axis=1, keepdims=True)
    lang_hot = (language[:, None] == jnp.arange(lang_count, dtype=jnp.int32)[None, :]).astype(
        jnp.float32
    )
    target = jnp.dot(lang_hot, teacher, precision=lax.Precision.HIGHEST)
    kd_dlogit = (scores - target).astype(jnp.bfloat16)
    slot_index = slots_of(picks, expert_count)
    position = picks.reshape(-1) * capacity + slot_index
    assign_rows = tok_dev * top_count
    slot_owner = (
        jnp.full((expert_count * capacity,), -1, jnp.int32)
        .at[position]
        .set(jnp.arange(assign_rows, dtype=jnp.int32))
    )
    is_valid = slot_owner >= 0
    token_of = jnp.maximum(slot_owner, 0) // top_count
    send_in = jnp.where(is_valid[:, None], tokens[token_of], jnp.zeros((), tokens.dtype)).reshape(
        expert_count, capacity, model_width
    )
    send_cot = jnp.where(
        is_valid[:, None], cotangent[token_of], jnp.zeros((), cotangent.dtype)
    ).reshape(expert_count, capacity, model_width)
    gate_w, up_w, down_w = (w_gate[0], w_up[0], w_down[0])
    got_in = lax.all_to_all(send_in, ("row", "col"), split_axis=0, concat_axis=0, tiled=True)
    got_cot = lax.all_to_all(send_cot, ("row", "col"), split_axis=0, concat_axis=0, tiled=True)
    sources, items, _ = got_in.shape
    grad_rows, pick_rows = expert_backward(
        got_in.reshape(sources * items, model_width),
        got_cot.reshape(sources * items, model_width),
        gate_w,
        up_w,
        down_w,
    )
    back_grad = lax.all_to_all(
        grad_rows.reshape(sources, items, model_width),
        ("row", "col"),
        split_axis=0,
        concat_axis=0,
        tiled=True,
    )
    back_pick = lax.all_to_all(
        pick_rows.reshape(sources, items), ("row", "col"), split_axis=0, concat_axis=0, tiled=True
    )
    gathered = back_grad.reshape(expert_count * capacity, model_width)[position].reshape(
        tok_dev, top_count, model_width
    )
    pick_back = back_pick.reshape(-1)[position].astype(jnp.float32).reshape(tok_dev, top_count)
    expert_sum = jnp.sum(route_w[:, :, None] * gathered, axis=1)
    mixed = jnp.sum(route_w * pick_back, axis=1, keepdims=True)
    per_pick = route_w * (1.0 - picked) * (pick_back - mixed / ROUTE_SCALE)
    pick_hot = (
        picks[:, :, None] == jnp.arange(expert_count, dtype=jnp.int32)[None, None, :]
    ).astype(jnp.float32)
    gate_dlogit = jnp.sum(per_pick[:, :, None] * pick_hot, axis=1).astype(jnp.bfloat16)
    router_part = jnp.dot(kd_dlogit, router.T, preferred_element_type=jnp.float32) + jnp.dot(
        gate_dlogit, router.T, preferred_element_type=jnp.float32
    )
    token_grad = (expert_sum + router_part).astype(jnp.bfloat16)
    router_share = lax.psum_scatter(
        column_term(tokens, kd_dlogit) + column_term(tokens, gate_dlogit),
        ("row", "col"),
        scatter_dimension=0,
        tiled=True,
    )
    router_grad = router_share / math.sqrt(total_tokens)
    return (token_grad, router_grad)


def solution(mesh):
    placed = (
        P(("row", "col"), None),
        P(("row", "col"), None),
        P(),
        P(("row", "col"), None),
        P(("row", "col")),
        P(),
        P(("row", "col"), None, None),
        P(("row", "col"), None, None),
        P(("row", "col"), None, None),
    )
    return jax.shard_map(
        local,
        mesh=mesh,
        in_specs=placed,
        out_specs=(P(("row", "col"), None), P(("row", "col"), None)),
        check_vma=False,
    )
```

profile of v0, /device:TPU:1, one launch (start us, length us, event | category | flops | bytes accessed | tf_op | source)
XLA Modules:
  0.0 412.5 jit_solution(11058028848764364611)
XLA Ops:
  7.2 0.9 copy.36
  8.2 0.7 broadcast_multiply_fusion
  9.7 1.4 scatter_custom_fusion
  11.2 3.9 gather_fusion
  15.0 6.8 %gather.22 = bf16[128,3,3584]{2,1,0:T(4,128)(2,1)} reshape(bf16[384,3584]{1,0:T(8,128)(2,1)} %gather_fusion) | data formatting | bytes 5505024 | tf_op jit(solution)/shard_map/gather | solution.py:77
  21.8 3.9 gather_fusion.1
  25.7 6.7 %gather.24 = bf16[128,3,3584]{2,1,0:T(4,128)(2,1)} reshape(bf16[384,3584]{1,0:T(8,128)(2,1)} %gather_fusion.1) | data formatting | bytes 5505024 | tf_op jit(solution)/shard_map/gather | solution.py:73
  32.6 7.0 %broadcast_select_fusion.1 = (bf16[128,3,3584]{2,1,0:T(4,128)(2,1)}, bf16[128,3,3584]{2,1,0:T(4,128)(2,1)S(1)}) fusion(bf16[128,3,3584]{2,1,0:T(4,128)(2,1)} %gather.22, pred[128,3]{1,0:T(8,128)(4,1)S(1)} %broadcast_in_dim.45, bf16[128,3,3584]{2,1,0:T(4,128)(2,1)} %gather.24), kind=kLoop, calls=%fused_computation.26 | loop fusion | flops 2752512 | bytes 11010432 | tf_op jit(solution)/shard_map/jit(_where)/select_n | solution.py:76
  39.6 58.9 %all_to_all.21 = bf16[128,3,3584]{2,1,0:T(4,128)(2,1)} all-to-all(bf16[128,3,3584]{2,1,0:T(4,128)(2,1)S(1)} %get-tuple-element.13), channel_id=1, replica_groups=mesh['row'=8,'col'=16] {'row','col'}, dimensions={0} | all-to-all | bytes 5505024 | tf_op jit(solution)/shard_map/all_to_all | solution.py:80
  98.5 5.3 %all-to-all-start = ((bf16[128,3,3584]{2,1,0:T(4,128)(2,1)}), bf16[128,3,3584]{2,1,0:T(4,128)(2,1)}, u32[]{:S(2)}, u32[]{:S(2)}) async-start(bf16[128,3,3584]{2,1,0:T(4,128)(2,1)} %get-tuple-element.12), calls=%async_computation | async-start | bytes 7340032 | tf_op jit(solution)/shard_map/all_to_all | solution.py:81
  104.2 1.9 gather_fusion.4
  106.3 7.1 %reshape.152 = bf16[384,3584]{1,0:T(8,128)(2,1)} reshape(bf16[128,3,3584]{2,1,0:T(4,128)(2,1)} %all_to_all.21) | data formatting | bytes 5505024 | tf_op jit(solution)/shard_map/reshape | solution.py:84
  113.5 6.1 %fusion.2 = f32[384,1024]{1,0:T(8,128)S(1)} fusion(bf16[384,3584]{1,0:T(8,128)(2,1)} %reshape.152, bf16[1,3584,1024]{2,1,0:T(8,128)(2,1)} %param.15), kind=kOutput, calls=%fused_computation.8 | convolution fusion | flops 2818572288 | bytes 11665408 | tf_op jit(solution)/shard_map/dot_general | solution.py:26
  119.5 31.7 %all-to-all-done = bf16[128,3,3584]{2,1,0:T(4,128)(2,1)} async-done(((bf16[128,3,3584]{2,1,0:T(4,128)(2,1)}), bf16[128,3,3584]{2,1,0:T(4,128)(2,1)}, u32[]{:S(2)}, u32[]{:S(2)}) %all-to-all-start) | async-done | bytes 2752544 | tf_op jit(solution)/shard_map/all_to_all | solution.py:81
  151.2 7.1 %reshape.151 = bf16[384,3584]{1,0:T(8,128)(2,1)} reshape(bf16[128,3,3584]{2,1,0:T(4,128)(2,1)} %all-to-all-done) | data formatting | bytes 5505024 | tf_op jit(solution)/shard_map/reshape | solution.py:85
  158.3 6.3 %fusion.8 = f32[384,1024]{1,0:T(8,128)S(1)} fusion(bf16[384,3584]{1,0:T(8,128)(2,1)} %reshape.151, bf16[1,1024,3584]{2,1,0:T(8,128)(2,1)} %param.17), kind=kOutput, calls=%fused_computation.14 | convolution fusion | flops 2818572288 | bytes 11665408 | tf_op jit(solution)/shard_map/dot_general | solution.py:28
  164.6 8.2 %multiply_reduce_fusion = (bf16[384]{0:T(512)(128)(2,1)S(1)}, f32[384,1024]{1,0:T(8,128)}) fusion(f32[384,1024]{1,0:T(8,128)S(1)} %fusion.8, f32[384,1024]{1,0:T(8,128)S(1)} %fusion.2, bf16[384,3584]{1,0:T(8,128)(2,1)S(1)} %copy-done.3, bf16[1,3584,1024]{2,1,0:T(8,128)(2,1)} %param.16), kind=kOutput, calls=%fused_computation.27 | convolution fusion | flops 2821324288 | bytes 14811904 | tf_op jit(solution)/shard_map/dot_general | solution.py:27
  172.8 0.9 convert_element_type.72
  173.7 4.2 %all-to-all-start.3 = ((bf16[128,1,3]{2,1,0:T(2,128)(2,1)}), bf16[128,1,3]{2,1,0:T(2,128)(2,1)S(1)}, u32[]{:S(2)}, u32[]{:S(2)}) async-start(bf16[128,1,3]{2,1,0:T(2,128)(2,1)} %convert_element_type.72), calls=%async_computation.3 | async-start | bytes 131072 | tf_op jit(solution)/shard_map/all_to_all | solution.py:97
  177.9 7.2 %fusion = f32[384,3584]{1,0:T(8,128)S(1)} fusion(bf16[1,3584,1024]{2,1,0:T(8,128)(2,1)} %param.15, f32[384,1024]{1,0:T(8,128)S(1)} %fusion.2, f32[384,1024]{1,0:T(8,128)} %copy-done.6, f32[384,1024]{1,0:T(8,128)} %get-tuple-element.15), kind=kOutput, calls=%fused_computation.6 | convolution fusion | flops 2822504448 | bytes 17563648 | tf_op jit(solution)/shard_map/dot_general | solution.py:34
  185.2 9.5 %fusion.13 = bf16[384,3584]{1,0:T(8,128)(2,1)} fusion(f32[384,3584]{1,0:T(8,128)S(1)} %fusion, bf16[1,3584,1024]{2,1,0:T(8,128)(2,1)} %param.16, f32[384,1024]{1,0:T(8,128)S(1)} %copy-done.7, f32[384,1024]{1,0:T(8,128)S(1)} %fusion.2), kind=kOutput, calls=%fused_computation.17 | convolution fusion | flops 2823684096 | bytes 18743296 | tf_op jit(solution)/shard_map/dot_general | solution.py:35
  194.6 6.7 %reshape.153 = bf16[128,3,3584]{2,1,0:T(4,128)(2,1)} reshape(bf16[384,3584]{1,0:T(8,128)(2,1)} %fusion.13) | data formatting | bytes 5505024 | tf_op jit(solution)/shard_map/reshape | solution.py:91
  201.4 10.3 %all-to-all-start.2 = ((bf16[128,3,3584]{2,1,0:T(4,128)(2,1)}), bf16[128,3,3584]{2,1,0:T(4,128)(2,1)}, u32[]{:S(2)}, u32[]{:S(2)}) async-start(bf16[128,3,3584]{2,1,0:T(4,128)(2,1)} %reshape.153), calls=%async_computation.2 | async-start | bytes 7340032 | tf_op jit(solution)/shard_map/all_to_all | solution.py:90
  213.0 1.9 gather_fusion.3
  215.5 1.7 fusion.16
  217.6 171.1 %all-reduce.3.cloned.1.call-done = f32[3584,128]{0,1:T(8,128)} async-done(((f32[3584,128]{0,1:T(8,128)}), f32[3584,128]{0,1:T(8,128)}) %all-reduce.3.cloned.1.call-update) | async-done | bytes 1835024
  388.7 1.0 dynamic-slice_multiply_fusion
  389.6 0.7 copy.46
  390.3 7.1 %reshape.154 = bf16[384,3584]{1,0:T(8,128)(2,1)} reshape(bf16[128,3,3584]{2,1,0:T(4,128)(2,1)} %all-to-all-done.2) | data formatting | bytes 5505024 | tf_op jit(solution)/shard_map/reshape | solution.py:100
  397.4 5.7 %gather_fusion.2 = bf16[256,3584]{1,0:T(8,128)(2,1)S(1)} fusion(bf16[384,3584]{1,0:T(8,128)(2,1)} %reshape.154, s32[1024]{0:T(1024)S(1)} %pad_clamp_fusion), kind=kCustom, calls=%fused_computation.2 | custom fusion | bytes 3671040 | tf_op jit(solution)/shard_map/gather | solution.py:100
  403.1 1.5 fusion.19
  404.5 1.1 fusion.18
  (55 shorter events, 4.0 us)
Async XLA Ops:
  7.2 96.8 %copy-start = (bf16[3584,128]{1,0:T(8,128)(2,1)S(1)}, bf16[3584,128]{1,0:T(8,128)(2,1)}, u32[]{:S(2)}) copy-start(bf16[3584,128]{1,0:T(8,128)(2,1)} %param.11) | copy-start | bytes 2752516
  7.2 4.0 copy-start.2
  15.0 6.8 %copy-start.1 = (bf16[32,3584]{1,0:T(8,128)(2,1)S(1)}, bf16[32,3584]{1,0:T(8,128)(2,1)}, u32[]{:S(2)}) copy-start(bf16[32,3584]{1,0:T(8,128)(2,1)} %param.9) | copy-start | bytes 688132
  98.5 52.7 %all-to-all-start = ((bf16[128,3,3584]{2,1,0:T(4,128)(2,1)}), bf16[128,3,3584]{2,1,0:T(4,128)(2,1)}, u32[]{:S(2)}, u32[]{:S(2)}) async-start(bf16[128,3,3584]{2,1,0:T(4,128)(2,1)} %get-tuple-element.12), calls=%async_computation | async-start | bytes 7340032 | tf_op jit(solution)/shard_map/all_to_all | solution.py:81
  158.3 6.3 %copy-start.3 = (bf16[384,3584]{1,0:T(8,128)(2,1)S(1)}, bf16[384,3584]{1,0:T(8,128)(2,1)}, u32[]{:S(2)}) copy-start(bf16[384,3584]{1,0:T(8,128)(2,1)} %reshape.152) | copy-start | bytes 8257540
  164.6 8.2 %copy-start.6 = (f32[384,1024]{1,0:T(8,128)}, f32[384,1024]{1,0:T(8,128)S(1)}, u32[]{:S(2)}) copy-start(f32[384,1024]{1,0:T(8,128)S(1)} %fusion.8) | copy-start | bytes 4718596
  173.7 27.7 %all-to-all-start.3 = ((bf16[128,1,3]{2,1,0:T(2,128)(2,1)}), bf16[128,1,3]{2,1,0:T(2,128)(2,1)S(1)}, u32[]{:S(2)}, u32[]{:S(2)}) async-start(bf16[128,1,3]{2,1,0:T(2,128)(2,1)} %convert_element_type.72), calls=%async_computation.3 | async-start | bytes 131072 | tf_op jit(solution)/shard_map/all_to_all | solution.py:97
  177.9 7.2 %copy-start.7 = (f32[384,1024]{1,0:T(8,128)S(1)}, f32[384,1024]{1,0:T(8,128)}, u32[]{:S(2)}) copy-start(f32[384,1024]{1,0:T(8,128)} %copy-done.6) | copy-start | bytes 4718596
  201.4 10.6 %copy-start.4 = (f32[8,128]{1,0:T(8,128)S(1)}, f32[8,128]{1,0:T(8,128)}, u32[]{:S(2)}) copy-start(f32[8,128]{1,0:T(8,128)} %param.14) | copy-start | bytes 12292
  201.4 10.6 %copy-start.5 = (s32[32]{0:T(128)S(1)}, s32[32]{0:T(128)}, u32[]{:S(2)}) copy-start(s32[32]{0:T(128)} %param.13) | copy-start | bytes 388
  201.4 189.0 %all-to-all-start.2 = ((bf16[128,3,3584]{2,1,0:T(4,128)(2,1)}), bf16[128,3,3584]{2,1,0:T(4,128)(2,1)}, u32[]{:S(2)}, u32[]{:S(2)}) async-start(bf16[128,3,3584]{2,1,0:T(4,128)(2,1)} %reshape.153), calls=%async_computation.2 | async-start | bytes 7340032 | tf_op jit(solution)/shard_map/all_to_all | solution.py:90
  211.7 177.0 %all-reduce.3.cloned.1.call-start = ((), (), s32[]{:S(2)}) async-start(), calls=%async_computation.4 | async-start | bytes 3670016
Sparse Core Ops, SparseCore 0:
  217.4 171.2 all-reduce.2
where the time goes:
time: 414 us; the launch traced here: 412 us
  waiting for transfers between devices  203 us (49%)
  local copies, waits for them, and re-layouts  63.6 us (15%)
  blocking collectives  58.9 us (14%)
  matrix products  41.4 us (10%)
  starting transfers between devices  20.1 us (5%)
  between operations  14.3 us (3%)
  other arithmetic  11.4 us (3%)
    unnamed x2, waiting for transfers between devices  171 us
    all_to_all x1, blocking collectives, local(): lax.all_to_all(send_in, ('row', 'col'), split_axis=0, concat_axis=0, tile...  58.9 us
    all_to_all x1, waiting for transfers between devices, local(): lax.all_to_all(send_cot, ('row', 'col'), split_axis=0, concat_axis=0, til...  31.7 us
    gather x2, local copies, waits for them, and re-layouts, local(): cotangent[token_of]  10.6 us
    gather x2, local copies, waits for them, and re-layouts, local(): tokens[token_of]  10.5 us
    all_to_all x1, starting transfers between devices, local(): lax.all_to_all(grad_rows.reshape(sources, items, model_width), ('row', 'c...  10.3 us
    dot_general x1, matrix products, expert_backward(): jnp.dot(up_grad, up_w.T, preferred_element_type=jnp.float32)  9.49 us
  transfers between devices with their start and end apart: 4, of which 2 were waited for; matrix products, arithmetic and copies ran while one was open for 11% of the time, Pallas kernels for 0%

commit v1 on v0

v1 whole, which is shorter than its diff:
```python
import math

import jax
import jax.numpy as jnp
import numpy as np
from jax import lax
from jax.experimental import pallas as pl
from jax.experimental.pallas import tpu as pltpu
from jax.sharding import PartitionSpec as P

D, FF, E, T, LANGS, TOP = 3584, 1024, 128, 32, 8, 8
ROUTE_SCALE = 2.5
MESH = pl.DeviceIdType.MESH
BF, F32 = jnp.bfloat16, jnp.float32
CHUNKS = ((0, 640), (1, 640), (2, 512))
BASE = tuple(sum(2 * c for _, c in CHUNKS[:i]) for i in range(len(CHUNKS)))
NC = len(CHUNKS)
ROWS = 384
NT = (((1,), (1,)), ((), ()))
TN = (((0,), (0,)), ((), ()))


def xyz_of(axis, u, v, w):
    return ((v, w, u), (v, u, w), (u, v, w))[axis]


def uvw_of(axis, x, y, z):
    return ((z, x, y), (y, x, z), (x, y, z))[axis]


def tables():
    perm = np.zeros((2, ROWS, ROWS), np.float32)
    for x in range(4):
        for y in range(4):
            for z in range(4):
                for s in range(6):
                    row = (x * 4 + y) * 24 + z * 6 + s
                    for axis in (1, 2):
                        u, v, w = uvw_of(axis, x, y, z)
                        perm[axis - 1, row, (v * 4 + w) * 24 + u * 6 + s] = 1
    select = np.zeros((2 * E, 12 * 128), np.float32)
    for axis in range(3):
        for u in range(4):
            for v in range(4):
                for w in range(4):
                    for k in range(2):
                        x, y, z = xyz_of(axis, u, v, w)
                        expert, j = 32 * z + 8 * x + 2 * y + k, v * 8 + w * 2 + k
                        at = (axis * 4 + u) * 128
                        select[expert, at + j] = 1
                        select[E + expert, at + 32 + j] = 1
    row, lane = np.arange(768)[:, None], np.arange(128)[None, :]
    spread = np.stack([row // 24 == lane, row // 24 + 32 == lane]).astype(np.float32)
    own, col = row % 24 // 3, np.arange(256)[None, :] // 32
    slot = np.where(own == col, row % 3 + 1, 9).astype(np.float32)
    short = np.arange(ROWS)[:, None]
    half = np.stack([short // 24 * 2 + k == lane for k in range(2)]).astype(np.float32)
    as_bf = lambda array: jnp.asarray(array, BF)
    return (as_bf(perm), as_bf(perm.transpose(0, 2, 1)), as_bf(select), as_bf(spread), as_bf(slot), as_bf(slot.T), as_bf(half))


def dot(a, b):
    return jnp.dot(a, b, preferred_element_type=F32)


def dot_nt(a, b):
    return lax.dot_general(a, b, NT, preferred_element_type=F32)


def dot_tn(a, b):
    return lax.dot_general(a, b, TN, preferred_element_type=F32)


def ident(x, y, z, k):
    return (z * 2 + x // 2, (x % 2) * 8 + y * 2 + k)


def kernel(
    tokens, cotangent, router, picks, language, teacher, w_gate, w_up, w_down,
    perm, perm_t, select, spread, slot, slot_t, half,
    token_grad, router_grad,
    wg, wu, wd, rows, meta_out, meta_in, pick_l, mix_w, r1, out2, x2, xt, xc, grads,
    yin, part, back, pg_out, pg_in, bp_out, bp_in, route, extra, rgs, rgb, rk, s1, rz, s2, rx, s3, ry,
    w_sem, in_sem, r1_s, r1_r, meta_s, meta_r, x2_s, x2_r, y_s, y_r, part_s, part_r, pg_s, pg_r, bp_s, bp_r, rg_s, rg_r,
):
    me_row, me_col = lax.axis_index("row"), lax.axis_index("col")
    x, y, z, k = (me_row % 2) * 2 + me_col // 8, (me_col // 2) % 4, me_row // 2, me_col % 2
    places = [uvw_of(axis, x, y, z) for axis in range(3)]

    def device(axis, u, v, w, core):
        return ident(*xyz_of(axis, u, v, w), core)

    def remote(src, dst, send, recv, where):
        return pltpu.make_async_remote_copy(
            src_ref=src, dst_ref=dst, send_sem=send, recv_sem=recv, device_id=where, device_id_type=MESH
        )

    def arrived(ref, sem):
        pltpu.make_async_copy(ref, ref, sem).wait()

    weights = [
        pltpu.make_async_copy(src.at[0], dst, w_sem.at[i])
        for i, (src, dst) in enumerate(((w_gate, wg), (w_up, wu), (w_down, wd)))
    ]
    inputs = [
        pltpu.make_async_copy(src, rows.at[i], in_sem.at[i]) for i, src in enumerate((tokens, cotangent))
    ]
    for copy in inputs + weights:
        copy.start()
    barrier = pltpu.get_barrier_semaphore()

    def greet(dx, dy, dz, dk):
        where = ident((x + dx) % 4, (y + dy) % 4, (z + dz) % 4, (k + dk) % 2)
        pl.semaphore_signal(barrier, inc=1, device_id=where, device_id_type=MESH)

    def greet_z(i, _):
        greet(i // 8, (i // 2) % 4, 0, i % 2)
        return 0

    def greet_y(i, _):
        greet(i // 6, 0, 1 + (i // 2) % 3, i % 2)
        return 0

    def greet_x(i, _):
        greet(0, 1 + i // 6, 1 + (i // 2) % 3, i % 2)
        return 0

    lax.fori_loop(1, 32, greet_z, 0)
    lax.fori_loop(0, 24, greet_y, 0)
    lax.fori_loop(0, 18, greet_x, 0)

    experts = lax.broadcasted_iota(jnp.int32, (T, E), 1)
    picked = jnp.zeros((T, E), F32)
    for i in range(TOP):
        picked += jnp.where(picks[:, i : i + 1] == experts, 1.0, 0.0)
    before = lax.broadcasted_iota(jnp.int32, (T, T), 1) < lax.broadcasted_iota(jnp.int32, (T, T), 0)
    rank = dot(jnp.where(before, 1.0, 0.0).astype(BF), picked.astype(BF))
    code = picked * (rank + 1.0)

    for copy in inputs:
        copy.wait()
    pl.semaphore_wait(barrier, 73)

    for i, (axis, wide) in enumerate(CHUNKS):
        u, v, w = places[axis]
        mine = u * 2 + k

        def hop(s, _, i=i, axis=axis, wide=wide, u=u, v=v, w=w, mine=mine):
            du, core = s // 2, (k + s) % 2
            start = pl.multiple_of(BASE[i] + core * wide, 128)
            remote(
                rows.at[:, :, pl.ds(start, wide)], r1[i].at[:, mine], r1_s.at[i], r1_r.at[i],
                device(axis, (u + du) % 4, v, w, core),
            ).start()
            return 0

        lax.fori_loop(1, 8, hop, 0)
        start = pl.multiple_of(BASE[i] + k * wide, 128)
        pltpu.make_async_copy(rows.at[:, :, pl.ds(start, wide)], r1[i].at[:, mine], r1_r.at[i]).start()

    logits = dot(rows[0], router[...])
    scores = jax.nn.sigmoid(logits)
    chosen = picked * scores
    weight = ROUTE_SCALE * chosen / jnp.sum(chosen, axis=1, keepdims=True)
    route[0] = weight
    route[1] = weight * (1.0 - scores)
    told = dot(code.astype(BF), select[0:E, :]) + dot(weight.astype(BF), select[E:, :])
    for m in range(12):
        meta_out[m] = told[:, m * 128 : (m + 1) * 128].astype(BF)
    for axis in range(3):
        u, v, w = places[axis]
        mine = u * 2 + k

        def tell(s, _, axis=axis, u=u, v=v, w=w, mine=mine):
            to = (u + s // 2) % 4
            core = (k + s) % 2
            remote(
                meta_out.at[axis * 4 + to], meta_in.at[axis, mine], meta_s.at[axis], meta_r.at[axis],
                device(axis, to, v, w, core),
            ).start()
            return 0

        lax.fori_loop(1, 8, tell, 0)
        pltpu.make_async_copy(meta_out.at[axis * 4 + u], meta_in.at[axis, mine], meta_r.at[axis]).start()

    target = jnp.zeros((T, E), F32)
    for i in range(LANGS):
        target += jnp.where(language[...] == i, teacher[i : i + 1, :], 0.0)
    route[2] = scores - target

    for i, (axis, wide) in enumerate(CHUNKS):
        arrived(meta_in.at[axis], meta_r.at[axis])
        codes = meta_in[axis].reshape(256, 128)
        pick_l[axis] = jnp.where(dot_nt(spread[0], codes) == slot[...].astype(F32), 1.0, 0.0).astype(BF)
        arrived(r1[i], r1_r.at[i])

        def gather(g, _, i=i, axis=axis, wide=wide):
            lhs = pick_l[axis, pl.ds(pl.multiple_of(g * 192, 192), 192), :]
            for a in range(2):
                got = dot(lhs, r1[i][a].reshape(256, wide)).astype(BF)
                out2[i][pl.ds(g * 8, 8), a * 24 : a * 24 + 24, :] = got.reshape(8, 24, wide)
            return 0

        lax.fori_loop(0, 4, gather, 0)

    def offsets(s):
        j = s % 16
        return j % 4, (j // 4 + j) % 4, s // 16

    def spread_out(s, _):
        dv, dw, dk = offsets(s)
        for i, (axis, wide) in enumerate(CHUNKS):
            u, v, w = places[axis]
            tv, tw, core = (v + dv) % 4, (w + dw) % 4, (k + dk) % 2
            remote(
                out2[i].at[tv * 8 + tw * 2 + core], x2[i].at[k, v * 4 + w], x2_s.at[i], x2_r.at[i],
                device(axis, u, tv, tw, core),
            ).start()
        return 0

    lax.fori_loop(1, 32, spread_out, 0)
    for i, (axis, wide) in enumerate(CHUNKS):
        u, v, w = places[axis]
        pltpu.make_async_copy(out2[i].at[v * 8 + w * 2 + k], x2[i].at[k, v * 4 + w], x2_r.at[i]).start()

    for axis in range(3):
        codes = meta_in[axis].reshape(256, 128)
        mix_w[axis] = jnp.where(
            dot_nt(codes, spread[0]) == slot_t[...].astype(F32), dot_nt(codes, spread[1]), 0.0
        ).astype(BF)

    for i, (axis, wide) in enumerate(CHUNKS):
        arrived(x2[i], x2_r.at[i])
        for q in range(2):
            cols = slice(BASE[i] + q * wide, BASE[i] + (q + 1) * wide)
            for a in range(2):
                got = x2[i][q, :, a * 24 : a * 24 + 24, :].reshape(ROWS, wide)
                got = got if axis == 0 else dot(perm[axis - 1], got).astype(BF)
                if a == 0:
                    xt[:, cols] = got
                else:
                    xc[:, :, cols] = got.reshape(16, 24, wide)
    for copy in weights:
        copy.wait()

    def hidden(n, total):
        cols = pl.ds(pl.multiple_of(n * 256, 256), 256)
        gate = dot(xt[...], wg[:, cols])
        up = dot(xt[...], wu[:, cols])
        into = dot_nt(xc[...].reshape(ROWS, D), wd[cols, :])
        sigma = jax.nn.sigmoid(gate)
        active = gate * sigma
        up_part = into * active
        grads[:, cols] = (into * up * (sigma * (1.0 + gate * (1.0 - sigma)))).astype(BF)
        grads[:, pl.ds(pl.multiple_of(FF + n * 256, 256), 256)] = up_part.astype(BF)
        return total + jnp.sum(up_part * up, axis=1, keepdims=True)

    pick_grad = lax.fori_loop(0, FF // 256, hidden, jnp.zeros((ROWS, 1), F32))
    pg_out[...] = jnp.broadcast_to(pick_grad, (ROWS, 128)).astype(BF).reshape(16, 24, 128)

    def send_pick(s, _):
        dv, dw, _ = offsets(s)
        tx, ty = (x + dv) % 4, (y + dw) % 4
        remote(pg_out.at[tx * 4 + ty], pg_in.at[x * 4 + y], pg_s, pg_r, ident(tx, ty, z, k)).start()
        return 0

    lax.fori_loop(1, 16, send_pick, 0)
    pltpu.make_async_copy(pg_out.at[x * 4 + y], pg_in.at[x * 4 + y], pg_r).start()

    for i, (axis, wide) in enumerate(CHUNKS):
        u, v, w = places[axis]
        if axis == 0:
            lhs = grads
        else:
            lhs = xt.at[:, 0 : 2 * FF]
            lhs[...] = dot(perm_t[axis - 1], grads[...]).astype(BF)
        for dq in range(2):
            q = (k + dq) % 2
            cols = pl.ds(pl.multiple_of(BASE[i] + q * wide, 128), wide)
            got = dot_nt(lhs[:, :FF], wg[cols, :]) + dot_nt(lhs[:, FF:], wu[cols, :])
            xc[:, :, cols] = got.astype(BF).reshape(16, 24, wide)

            def give(s, _, i=i, axis=axis, u=u, v=v, w=w, q=q, cols=cols):
                dv, dw, _ = offsets(s)
                tv, tw = (v + dv) % 4, (w + dw) % 4
                remote(
                    xc.at[tv * 4 + tw, :, cols], yin[i].at[v * 8 + w * 2 + k], y_s.at[i], y_r.at[i],
                    device(axis, u, tv, tw, q),
                ).start()
                return 0

            lax.fori_loop(1 - dq, 16, give, 0)
            if dq == 0:
                pltpu.make_async_copy(xc.at[v * 4 + w, :, cols], yin[i].at[v * 8 + w * 2 + k], y_r.at[i]).start()

    arrived(pg_in, pg_r)
    codes = meta_in[0].reshape(256, 128)
    wanted = jnp.where(dot_nt(codes, half[k]) == slot_t[:, :ROWS].astype(F32), 1.0, 0.0).astype(BF)
    line = lax.broadcasted_iota(jnp.int32, (ROWS, 128), 0)
    owner = 32 * z + 2 * ((line * 2731) >> 16) + k
    values = jnp.where(
        lax.broadcasted_iota(jnp.int32, (ROWS, 128), 1) == owner, pg_in[...].reshape(ROWS, 128).astype(F32), 0.0
    ).astype(BF)
    bp_out[...] = dot(wanted, values).astype(BF).reshape(8, T, 128)

    def send_dense(s, _):
        to, core = (z + s // 2) % 4, (k + s) % 2
        remote(bp_out.at[to * 2 + core], bp_in.at[z * 2 + k], bp_s, bp_r, ident(x, y, to, core)).start()
        return 0

    lax.fori_loop(1, 8, send_dense, 0)
    pltpu.make_async_copy(bp_out.at[z * 2 + k], bp_in.at[z * 2 + k], bp_r).start()

    arrived(bp_in, bp_r)
    pick_back = jnp.sum(bp_in[...].astype(F32), axis=0)
    mixed = jnp.sum(route[0] * pick_back, axis=1, keepdims=True)
    gate_dlogit = (route[1] * (pick_back - mixed / ROUTE_SCALE)).astype(BF)
    kd_dlogit = route[2].astype(BF)
    extra[...] = dot_nt(kd_dlogit, router[...]) + dot_nt(gate_dlogit, router[...])

    rgs[896:, :] = jnp.zeros((8, 128), F32)
    for zq in range(4):
        mine = rows[0, :, zq * 896 : (zq + 1) * 896]
        rgs[0:896, :] = dot_tn(mine, kd_dlogit) + dot_tn(mine, gate_dlogit)
        for g in range(32):
            rgb[g % 2, zq * 16 + g // 2] = rgs[28 * g : 28 * g + 32, :].astype(BF)
    to_core = remote(rgb.at[1 - k], rk, rg_s.at[0], rg_r.at[0], ident(x, y, z, 1 - k))
    to_core.start()

    def combine(i):
        axis, wide = CHUNKS[i]
        u, v, w = places[axis]
        arrived(yin[i], y_r.at[i])
        part[i][...] = dot(mix_w[axis], yin[i][...].reshape(768, wide)).astype(BF).reshape(8, T, wide)

        def give_back(s, _):
            to, core = (u + s // 2) % 4, (k + s) % 2
            remote(
                part[i].at[to * 2 + core], back[i].at[k, u], part_s.at[i], part_r.at[i], device(axis, to, v, w, core)
            ).start()
            return 0

        lax.fori_loop(1, 8, give_back, 0)
        pltpu.make_async_copy(part[i].at[u * 2 + k], back[i].at[k, u], part_r.at[i]).start()

    to_core.wait_recv()
    s1[...] = (rgb[k].astype(F32) + rk[...].astype(F32)).astype(BF)

    def scatter(source, count, into, at, step, where):
        def one(d, _):
            to = (at + d) % 4
            remote(
                source.at[pl.ds(to * count, count)], into.at[at], rg_s.at[step], rg_r.at[step], where(to)
            ).start()
            return 0

        lax.fori_loop(1, 4, one, 0)
        pltpu.make_async_copy(source.at[pl.ds(at * count, count)], into.at[at], rg_r.at[step]).start()

    scatter(s1, 16, rz, z, 1, lambda to: ident(x, y, to, k))
    combine(0)
    arrived(rz, rg_r.at[1])
    s2[...] = jnp.sum(rz[...].astype(F32), axis=0)
    scatter(s2, 4, rx, x, 2, lambda to: ident(to, y, z, k))
    combine(1)
    arrived(rx, rg_r.at[2])
    s3[...] = jnp.sum(rx[...], axis=0)
    scatter(s3, 1, ry, y, 3, lambda to: ident(x, to, z, k))
    combine(2)
    arrived(ry, rg_r.at[3])
    router_grad[...] = jnp.sum(ry[...], axis=(0, 1))[:28, :] / math.sqrt(E * T)

    for i, (axis, wide) in enumerate(CHUNKS):
        arrived(back[i], part_r.at[i])
        for q in range(2):
            cols = slice(BASE[i] + q * wide, BASE[i] + (q + 1) * wide)
            token_grad[:, cols] = (jnp.sum(back[i][q].astype(F32), axis=0) + extra[:, cols]).astype(BF)

    for i in range(NC):
        arrived(r1[i].at[:, pl.ds(0, 7)], r1_s.at[i])
        arrived(x2[i].at[0], x2_s.at[i])
        arrived(x2[i].at[0, pl.ds(0, 15)], x2_s.at[i])
        arrived(yin[i].at[pl.ds(0, 31)], y_s.at[i])
        arrived(part[i].at[pl.ds(0, 7)], part_s.at[i])
    for axis in range(3):
        arrived(meta_in.at[axis, pl.ds(0, 7)], meta_s.at[axis])
    arrived(pg_in.at[pl.ds(0, 15)], pg_s)
    arrived(bp_in.at[pl.ds(0, 7)], bp_s)
    to_core.wait_send()
    arrived(rz.at[pl.ds(0, 3)], rg_s.at[1])
    arrived(rx.at[pl.ds(0, 3)], rg_s.at[2])
    arrived(ry.at[pl.ds(0, 3)], rg_s.at[3])


def local(tokens, cotangent, router, picks, language, teacher, w_gate, w_up, w_down):
    vmem, anywhere = pl.BlockSpec(memory_space=pltpu.VMEM), pl.BlockSpec(memory_space=pl.ANY)
    buf, sem = pltpu.VMEM, pltpu.SemaphoreType.DMA
    per = lambda make: tuple(buf(make(wide), BF) for _, wide in CHUNKS)
    scratch = [
        buf((D, FF), BF), buf((D, FF), BF), buf((FF, D), BF),
        buf((2, T, D), BF),
        buf((12, T, 128), BF), buf((3, 8, T, 128), BF),
        buf((3, 768, 256), BF), buf((3, 256, 768), BF),
        per(lambda c: (2, 8, T, c)),
        per(lambda c: (32, 48, c)), per(lambda c: (2, 16, 48, c)),
        buf((ROWS, D), BF), buf((16, 24, D), BF),
        buf((ROWS, 2 * FF), BF),
        per(lambda c: (32, 24, c)),
        per(lambda c: (8, T, c)), per(lambda c: (2, 4, T, c)),
        buf((16, 24, 128), BF), buf((16, 24, 128), BF),
        buf((8, T, 128), BF), buf((8, T, 128), BF),
        buf((3, T, E), F32), buf((T, D), F32),
        buf((904, 128), F32), buf((2, 64, 32, 128), BF), buf((64, 32, 128), BF),
        buf((64, 32, 128), BF), buf((4, 16, 32, 128), BF),
        buf((16, 32, 128), F32), buf((4, 4, 32, 128), F32),
        buf((4, 32, 128), F32), buf((4, 1, 32, 128), F32),
        sem((3,)), sem((2,)),
        sem((NC,)), sem((NC,)), sem((3,)), sem((3,)), sem((NC,)), sem((NC,)), sem((NC,)), sem((NC,)), sem((NC,)), sem((NC,)),
        sem, sem, sem, sem, sem((4,)), sem((4,)),
    ]
    return pl.pallas_call(
        kernel,
        out_shape=(jax.ShapeDtypeStruct((T, D), BF), jax.ShapeDtypeStruct((28, 128), F32)),
        in_specs=[anywhere, anywhere, vmem, vmem, vmem, vmem, anywhere, anywhere, anywhere] + [vmem] * 7,
        out_specs=(vmem, vmem),
        scratch_shapes=scratch,
        compiler_params=pltpu.CompilerParams(
            collective_id=0, has_side_effects=True, vmem_limit_bytes=60 << 20
        ),
        cost_estimate=pl.CostEstimate(flops=15_000_000_000, bytes_accessed=24_000_000, transcendentals=400_000),
    )(tokens, cotangent, router, picks, language.reshape(T, 1), teacher, w_gate, w_up, w_down, *tables())


def solution(mesh):
    split = P(("row", "col"), None)
    cube = P(("row", "col"), None, None)
    return jax.shard_map(
        local,
        mesh=mesh,
        in_specs=(split, split, P(), split, P(("row", "col")), P(), cube, cube, cube),
        out_specs=(split, split),
        check_vma=False,
    )
```

time: 414 us -> 149 us (0.36)
  waiting for transfers between devices: 203 us -> 0 us
  Pallas kernels: 0 us -> 142 us
  blocking collectives: 58.9 us -> 0 us
  local copies, waits for them, and re-layouts: 63.6 us -> 5.67 us
  matrix products: 41.4 us -> 0 us
  starting transfers between devices: 20.1 us -> 0 us
  between operations: 14.3 us -> 0.64 us
  other arithmetic: 11.4 us -> 0 us
    unnamed x2 -> x0, waiting for transfers between devices: 171 us -> none
    pallas_call x0 -> x1, Pallas kernels: none -> 142 us  [local(): pl.pallas_call(kernel, out_shape=(jax.ShapeDtypeStruct((T, D), BF), jax.S...]
    all_to_all x1 -> x0, blocking collectives: 58.9 us -> none  [local(): lax.all_to_all(send_in, ('row', 'col'), split_axis=0, concat_axis=0, tile...]
    dot_general x11 -> x0, matrix products: 41.4 us -> none  [the longest x1 9.49 us: expert_backward(): jnp.dot(up_grad, up_w.T, preferred_element_type=jnp.float32)]
    all_to_all x3 -> x0, waiting for transfers between devices: 31.7 us -> none  [the longest x1 31.7 us: local(): lax.all_to_all(send_cot, ('row', 'col'), split_axis=0, concat_axis=0, til...]
    gather x9 -> x0, local copies, waits for them, and re-layouts: 30.8 us -> none  [the longest x2 10.6 us: local(): cotangent[token_of]]
    reshape x5 -> x1, local copies, waits for them, and re-layouts: 28.1 us -> 1.34 us  [local(): language.reshape(T, 1)]
    all_to_all x3 -> x0, starting transfers between devices: 19.8 us -> none  [the longest x1 10.3 us: local(): lax.all_to_all(grad_rows.reshape(sources, items, model_width), ('row', 'c...]
  transfers between devices with their start and end apart: 4 -> 0, of which waited for: 2 -> 0; matrix products, arithmetic and copies ran while one was open for 11% -> 0% of each run, Pallas kernels for 0% -> 0%
where the time goes in v1:
time: 149 us
  Pallas kernels  142 us (95%)
  local copies, waits for them, and re-layouts  5.67 us (4%)
    pallas_call x1, Pallas kernels, local(): pl.pallas_call(kernel, out_shape=(jax.ShapeDtypeStruct((T, D), BF), jax.S...  142 us
    unnamed x3, local copies, waits for them, and re-layouts  4.33 us

profile of v1, /device:TPU:1, one launch (start us, length us, event | category | flops | bytes accessed | tf_op | source)
XLA Modules:
  0.0 148.7 jit_solution(2477525971269528718)
XLA Ops:
  0.6 1.4 copy.18.picks
  2.0 1.3 copy.19.language
  3.3 142.4 %shard_map.167 = (bf16[32,3584]{1,0:T(8,128)(2,1)}, f32[28,128]{1,0:T(8,128)}) custom-call(bf16[32,3584]{1,0:T(8,128)(2,1)} %tokens.1, bf16[32,3584]{1,0:T(8,128)(2,1)} %cotangent.1, bf16[3584,128]{1,0:T(8,128)(2,1)} %router.1, s32[32,8]{1,0:T(8,128)} %copy.18.picks, s32[32,1]{1,0:T(8,128)} %copy.19.language, f32[8,128]{1,0:T(8,128)} %teacher.1, ...), custom_call_target="tpu_custom_call" | custom-call | flops 15000000512 | bytes 24000000 | tf_op jit(solution)/shard_map/pallas_call | solution.py:421
  145.8 1.6 %copy.22 = bf16[32,3584]{1,0:T(8,128)(2,1)} copy(bf16[32,3584]{1,0:T(8,128)(2,1)} %get-tuple-element.4) | data formatting | bytes 458752
  147.4 1.3 copy.23

commit v2 on v1

v2 whole, which is shorter than its diff:
```python
import math

import jax
import jax.numpy as jnp
import numpy as np
from jax import lax
from jax.experimental import pallas as pl
from jax.experimental.pallas import tpu as pltpu
from jax.sharding import PartitionSpec as P

D, FF, E, T, LANGS, TOP = 3584, 1024, 128, 32, 8, 8
ROUTE_SCALE = 2.5
MESH = pl.DeviceIdType.MESH
BF, F32 = jnp.bfloat16, jnp.float32
CHUNKS = ((0, 128), (1, 128), (2, 128), (0, 384), (1, 384), (2, 256), (0, 128), (1, 128), (2, 128))
SETS = ((0, 1, 2), (3, 4, 5), (6, 7, 8))
BASE = tuple(sum(2 * c for _, c in CHUNKS[:i]) for i in range(len(CHUNKS)))
NC = len(CHUNKS)
RETURN = ((0, 512), (1, 512), (2, 384), (0, 128), (1, 128), (2, 128))
RBASE = tuple(sum(2 * c for _, c in RETURN[:i]) for i in range(len(RETURN)))
NR = len(RETURN)
ROWS = 384
FIRST = BASE[SETS[2][0]]
NT = (((1,), (1,)), ((), ()))
TN = (((0,), (0,)), ((), ()))


def xyz_of(axis, u, v, w):
    return ((v, w, u), (v, u, w), (u, v, w))[axis]


def uvw_of(axis, x, y, z):
    return ((z, x, y), (y, x, z), (x, y, z))[axis]


def tables():
    perm = np.zeros((2, ROWS, ROWS), np.float32)
    for x in range(4):
        for y in range(4):
            for z in range(4):
                for s in range(6):
                    row = (x * 4 + y) * 24 + z * 6 + s
                    for axis in (1, 2):
                        u, v, w = uvw_of(axis, x, y, z)
                        perm[axis - 1, row, (v * 4 + w) * 24 + u * 6 + s] = 1
    select = np.zeros((2 * E, 12 * 128), np.float32)
    for axis in range(3):
        for u in range(4):
            for v in range(4):
                for w in range(4):
                    for k in range(2):
                        x, y, z = xyz_of(axis, u, v, w)
                        expert, j = 32 * z + 8 * x + 2 * y + k, v * 8 + w * 2 + k
                        at = (axis * 4 + u) * 128
                        select[expert, at + j] = 1
                        select[E + expert, at + 32 + j] = 1
    row, lane = np.arange(768)[:, None], np.arange(128)[None, :]
    eye = np.eye(E, dtype=np.float32)
    spread = np.stack([row // 24 == lane, row // 24 + 32 == lane]).astype(np.float32)
    own, col = row % 24 // 3, np.arange(256)[None, :] // 32
    slot = np.where(own == col, row % 3 + 1, 9).astype(np.float32)
    short = np.arange(ROWS)[:, None]
    half = np.stack([short // 24 * 2 + k == lane for k in range(2)]).astype(np.float32)
    as_bf = lambda array: jnp.asarray(array, BF)
    return (as_bf(perm), as_bf(select), as_bf(spread), as_bf(slot[:24]), as_bf(slot[:ROWS].T), as_bf(half), as_bf(eye))


def dot(a, b):
    return jnp.dot(a, b, preferred_element_type=F32)


def dot_nt(a, b):
    return lax.dot_general(a, b, NT, preferred_element_type=F32)


def dot_tn(a, b):
    return lax.dot_general(a, b, TN, preferred_element_type=F32)


def ident(x, y, z, k):
    return (z * 2 + x // 2, (x % 2) * 8 + y * 2 + k)


def kernel(
    tokens, cotangent, router, picks, language, teacher, w_gate, w_up, w_down,
    perm, select_hbm, spread, slot, slot_t, half, eye,
    token_grad, router_grad,
    wg, wu, wd, rows, meta_out, meta_in, pick_l, mix_w, r1, out2, x2, xt, xc, acc, grads,
    yin, part, back, pg_out, pg_in, bp_out, bp_in, route, extra, rgs, rgb, rk, s1, rz, s2, rx,
    ready, w_sem, in_sem, r1_s, r1_r, meta_s, meta_r, x2_s, x2_r, y_s, y_r, part_s, part_r, pg_s, pg_r, bp_s, bp_r, rg_s, rg_r,
):
    me_row, me_col = lax.axis_index("row"), lax.axis_index("col")
    x, y, z, k = (me_row % 2) * 2 + me_col // 8, (me_col // 2) % 4, me_row // 2, me_col % 2
    places = [uvw_of(axis, x, y, z) for axis in range(3)]

    def device(axis, u, v, w, core):
        return ident(*xyz_of(axis, u, v, w), core)

    def remote(src, dst, send, recv, where):
        return pltpu.make_async_remote_copy(
            src_ref=src, dst_ref=dst, send_sem=send, recv_sem=recv, device_id=where, device_id_type=MESH
        )

    def arrived(ref, sem):
        pltpu.make_async_copy(ref, ref, sem).wait()

    weights = [
        pltpu.make_async_copy(src.at[0], dst, w_sem.at[i])
        for i, (src, dst) in enumerate(((w_gate, wg), (w_up, wu), (w_down, wd)))
    ]
    select = xt.at[0 : 2 * E, 0 : 12 * 128]
    inputs = [
        pltpu.make_async_copy(src, dst, in_sem.at[i])
        for i, (src, dst) in enumerate(((tokens, rows.at[0]), (cotangent, rows.at[1]), (select_hbm, select)))
    ]
    for copy in inputs + weights:
        copy.start()
    barrier = pltpu.get_barrier_semaphore()

    def greet(sem):
        for axis in range(3):
            u, v, w = places[axis]

            def one(s, _, axis=axis, u=u, v=v, w=w):
                where = device(axis, (u + s // 2) % 4, v, w, (k + s) % 2)
                pl.semaphore_signal(sem, inc=1, device_id=where, device_id_type=MESH)
                return 0

            lax.fori_loop(2 if axis else 1, 8, one, 0)

    greet(barrier)

    experts = lax.broadcasted_iota(jnp.int32, (E, T), 0)
    asked = jnp.zeros((E, T), F32)
    for i in range(TOP):
        asked += jnp.where(picks[i : i + 1, :] == experts, 1.0, 0.0)
    before = lax.broadcasted_iota(jnp.int32, (T, T), 0) < lax.broadcasted_iota(jnp.int32, (T, T), 1)
    rank = dot(asked.astype(BF), jnp.where(before, 1.0, 0.0).astype(BF))
    code = dot_tn((asked * (rank + 1.0)).astype(BF), eye[...])
    picked = jnp.where(code > 0.0, 1.0, 0.0)
    spoken = jnp.where(lax.broadcasted_iota(jnp.int32, (LANGS, T), 0) == language[...], 1.0, 0.0).astype(BF)
    target, left = jnp.zeros((T, E), F32), teacher[...]
    for _ in range(3):
        piece = left.astype(BF)
        left = left - piece.astype(F32)
        target += dot_tn(spoken, piece)

    for copy in inputs:
        copy.wait()
    logits = dot(rows[0], router[...])
    scores = jax.nn.sigmoid(logits)
    chosen = picked * scores
    weight = ROUTE_SCALE * chosen / jnp.sum(chosen, axis=1, keepdims=True)
    route[0] = weight
    route[1] = weight * (1.0 - scores)
    route[2] = scores - target
    told = dot(code.astype(BF), select[0:E, :]) + dot(weight.astype(BF), select[E:, :])
    for m in range(12):
        meta_out[m] = told[:, m * 128 : (m + 1) * 128].astype(BF)
    pl.semaphore_wait(barrier, 19)
    greet(ready)

    for axis in range(3):
        u, v, w = places[axis]
        mine = u * 2 + k

        def tell(s, _, axis=axis, u=u, v=v, w=w, mine=mine):
            to = (u + s // 2) % 4
            core = (k + s) % 2
            remote(
                meta_out.at[axis * 4 + to], meta_in.at[axis, mine], meta_s.at[axis], meta_r.at[axis],
                device(axis, to, v, w, core),
            ).start()
            return 0

        lax.fori_loop(1, 8, tell, 0)
        pltpu.make_async_copy(meta_out.at[axis * 4 + u], meta_in.at[axis, mine], meta_r.at[axis]).start()

    for i, (axis, wide) in enumerate(CHUNKS):
        u, v, w = places[axis]
        mine = u * 2 + k

        def hop(s, _, i=i, axis=axis, wide=wide, u=u, v=v, w=w, mine=mine):
            du, core = s // 2, (k + s) % 2
            start = pl.multiple_of(BASE[i] + core * wide, 128)
            remote(
                rows.at[:, :, pl.ds(start, wide)], r1[i].at[:, mine], r1_s.at[i], r1_r.at[i],
                device(axis, (u + du) % 4, v, w, core),
            ).start()
            return 0

        lax.fori_loop(1, 8, hop, 0)
        start = pl.multiple_of(BASE[i] + k * wide, 128)
        pltpu.make_async_copy(rows.at[:, :, pl.ds(start, wide)], r1[i].at[:, mine], r1_r.at[i]).start()

    def offsets(s):
        j = s % 16
        return j % 4, (j // 4 + j) % 4, s // 16

    for axis in range(3):
        arrived(meta_in.at[axis], meta_r.at[axis])
        codes = meta_in[axis].reshape(256, 128)
        slots = jnp.broadcast_to(slot[...].astype(F32)[None], (32, 24, 256)).reshape(768, 256)
        pick_l[axis] = jnp.where(dot_nt(spread[0], codes) == slots, 1.0, 0.0).astype(BF)

    def relay(chunks):
        for i in chunks:
            axis, wide = CHUNKS[i]
            arrived(r1[i], r1_r.at[i])

            def gather(g, _, i=i, axis=axis, wide=wide):
                lhs = pick_l[axis, pl.ds(pl.multiple_of(g * 192, 192), 192), :]
                for a in range(2):
                    got = dot(lhs, r1[i][a].reshape(256, wide)).astype(BF)
                    out2[i][pl.ds(g * 8, 8), a * 24 : a * 24 + 24, :] = got.reshape(8, 24, wide)
                return 0

            lax.fori_loop(0, 4, gather, 0)

        if chunks == SETS[0]:
            pl.semaphore_wait(ready, 19)

        def spread_out(s, _):
            dv, dw, dk = offsets(s)
            for i in chunks:
                axis, wide = CHUNKS[i]
                u, v, w = places[axis]
                tv, tw, core = (v + dv) % 4, (w + dw) % 4, (k + dk) % 2
                remote(
                    out2[i].at[tv * 8 + tw * 2 + core], x2[i].at[k, v * 4 + w], x2_s.at[i], x2_r.at[i],
                    device(axis, u, tv, tw, core),
                ).start()
            return 0

        lax.fori_loop(1, 32, spread_out, 0)
        for i in chunks:
            u, v, w = places[CHUNKS[i][0]]
            pltpu.make_async_copy(out2[i].at[v * 8 + w * 2 + k], x2[i].at[k, v * 4 + w], x2_r.at[i]).start()

    for chunks in SETS:
        relay(chunks)

    slots_t = jnp.concatenate([slot_t[...].astype(F32)] * 2, axis=1)
    for axis in range(3):
        codes = meta_in[axis].reshape(256, 128)
        mix_w[axis] = jnp.where(dot_nt(codes, spread[0]) == slots_t, dot_nt(codes, spread[1]), 0.0).astype(BF)

    def collect(chunks):
        for i in chunks:
            axis, wide = CHUNKS[i]
            arrived(x2[i], x2_r.at[i])
            for q in range(2):
                cols = slice(BASE[i] + q * wide, BASE[i] + (q + 1) * wide)
                for a in range(2):
                    got = x2[i][q, :, a * 24 : a * 24 + 24, :].reshape(ROWS, wide)
                    got = got if axis == 0 else dot(perm[axis - 1], got).astype(BF)
                    if a == 0:
                        xt[:, cols] = got
                    else:
                        xc[:, :, cols] = got.reshape(16, 24, wide)

    def parts(n, low, high):
        cols = pl.ds(pl.multiple_of(n * 256, 256), 256)
        gate = dot(xt[:, low:high], wg[low:high, cols])
        up = dot(xt[:, low:high], wu[low:high, cols])
        into = dot_nt(xc[:, :, low:high].reshape(ROWS, high - low), wd[cols, low:high])
        return cols, gate, up, into

    def first(n, _):
        cols, *values = parts(n, 0, FIRST)
        for i, value in enumerate(values):
            acc[i, :, cols] = value
        return 0

    def second(n, total):
        cols, gate, up, into = parts(n, FIRST, D)
        gate, up, into = acc[0, :, cols] + gate, acc[1, :, cols] + up, acc[2, :, cols] + into
        sigma = jax.nn.sigmoid(gate)
        active = gate * sigma
        up_part = into * active
        grads[:, cols] = (into * up * (sigma * (1.0 + gate * (1.0 - sigma)))).astype(BF)
        grads[:, pl.ds(pl.multiple_of(FF + n * 256, 256), 256)] = up_part.astype(BF)
        return total + jnp.sum(up_part * up, axis=1, keepdims=True)

    collect(SETS[0])
    collect(SETS[1])
    for copy in weights:
        copy.wait()
    lax.fori_loop(0, FF // 256, first, 0)
    collect(SETS[2])
    pick_grad = lax.fori_loop(0, FF // 256, second, jnp.zeros((ROWS, 1), F32))
    pg_out[...] = jnp.broadcast_to(pick_grad, (ROWS, 128)).astype(BF).reshape(16, 24, 128)

    def send_pick(s, _):
        dv, dw, _ = offsets(s)
        tx, ty = (x + dv) % 4, (y + dw) % 4
        remote(pg_out.at[tx * 4 + ty], pg_in.at[x * 4 + y], pg_s, pg_r, ident(tx, ty, z, k)).start()
        return 0

    lax.fori_loop(1, 16, send_pick, 0)
    pltpu.make_async_copy(pg_out.at[x * 4 + y], pg_in.at[x * 4 + y], pg_r).start()

    def permute(axis):
        if axis:
            xt[:, 0 : 2 * FF] = dot_tn(perm[axis - 1], grads[...]).astype(BF)

    def produce(i, dq):
        axis, wide = RETURN[i]
        cols = pl.ds(pl.multiple_of(RBASE[i] + (k + dq) % 2 * wide, 128), wide)
        lhs = xt if axis else grads
        got = dot_nt(lhs[:, :FF], wg[cols, :]) + dot_nt(lhs[:, FF : 2 * FF], wu[cols, :])
        xc[:, :, cols] = got.astype(BF).reshape(16, 24, wide)

    def give(i, dq):
        axis, wide = RETURN[i]
        u, v, w = places[axis]
        q = (k + dq) % 2
        cols = pl.ds(pl.multiple_of(RBASE[i] + q * wide, 128), wide)

        def one(s, _):
            dv, dw, _ = offsets(s)
            tv, tw = (v + dv) % 4, (w + dw) % 4
            remote(
                xc.at[tv * 4 + tw, :, cols], yin[i].at[v * 8 + w * 2 + k], y_s.at[i], y_r.at[i],
                device(axis, u, tv, tw, q),
            ).start()
            return 0

        lax.fori_loop(1 - dq, 16, one, 0)
        if dq == 0:
            pltpu.make_async_copy(xc.at[v * 4 + w, :, cols], yin[i].at[v * 8 + w * 2 + k], y_r.at[i]).start()

    def whole(i):
        for dq in range(2):
            produce(i, dq)
            give(i, dq)

    def combine(i):
        axis, wide = RETURN[i]
        u, v, w = places[axis]
        arrived(yin[i], y_r.at[i])
        part[i][...] = dot(mix_w[axis], yin[i][...].reshape(768, wide)).astype(BF).reshape(8, T, wide)

        def give_back(s, _):
            to, core = (u + s // 2) % 4, (k + s) % 2
            remote(
                part[i].at[to * 2 + core], back[i].at[k, u], part_s.at[i], part_r.at[i], device(axis, to, v, w, core)
            ).start()
            return 0

        lax.fori_loop(1, 8, give_back, 0)
        pltpu.make_async_copy(part[i].at[u * 2 + k], back[i].at[k, u], part_r.at[i]).start()

    produce(0, 0)
    give(0, 0)
    produce(0, 1)
    give(0, 1)

    arrived(pg_in, pg_r)
    codes = meta_in[0].reshape(256, 128)
    wanted = jnp.where(dot_nt(codes, half[k]) == slot_t[...].astype(F32), 1.0, 0.0).astype(BF)
    line = lax.broadcasted_iota(jnp.int32, (ROWS, 128), 0)
    owner = 32 * z + 2 * ((line * 2731) >> 16) + k
    values = jnp.where(
        lax.broadcasted_iota(jnp.int32, (ROWS, 128), 1) == owner, pg_in[...].reshape(ROWS, 128).astype(F32), 0.0
    ).astype(BF)
    bp_out[...] = dot(wanted, values).astype(BF).reshape(8, T, 128)

    def send_dense(s, _):
        to, core = (z + s // 2) % 4, (k + s) % 2
        remote(bp_out.at[to * 2 + core], bp_in.at[z * 2 + k], bp_s, bp_r, ident(x, y, to, core)).start()
        return 0

    lax.fori_loop(1, 8, send_dense, 0)
    pltpu.make_async_copy(bp_out.at[z * 2 + k], bp_in.at[z * 2 + k], bp_r).start()

    whole(3)
    permute(1)
    whole(1)
    whole(4)

    arrived(bp_in, bp_r)
    pick_back = jnp.sum(bp_in[...].astype(F32), axis=0)
    mixed = jnp.sum(route[0] * pick_back, axis=1, keepdims=True)
    gate_dlogit = (route[1] * (pick_back - mixed / ROUTE_SCALE)).astype(BF)
    kd_dlogit = route[2].astype(BF)

    rgs[896:, :] = jnp.zeros((8, 128), F32)
    for zq in range(4):
        mine = rows[0, :, zq * 896 : (zq + 1) * 896]
        rgs[0:896, :] = dot_tn(mine, kd_dlogit) + dot_tn(mine, gate_dlogit)
        for g in range(32):
            rgb[g % 2, zq * 16 + g // 2] = rgs[28 * g : 28 * g + 32, :].astype(BF)
    to_core = remote(rgb.at[1 - k], rk, rg_s.at[0], rg_r.at[0], ident(x, y, z, 1 - k))
    to_core.start()

    permute(2)
    whole(2)
    whole(5)
    to_core.wait_recv()
    s1[...] = (rgb[k].astype(F32) + rk[...].astype(F32)).astype(BF)

    def to_plane(d, _):
        to = (z + d) % 4
        remote(s1.at[pl.ds(to * 16, 16)], rz.at[z], rg_s.at[1], rg_r.at[1], ident(x, y, to, k)).start()
        return 0

    lax.fori_loop(1, 4, to_plane, 0)
    pltpu.make_async_copy(s1.at[pl.ds(z * 16, 16)], rz.at[z], rg_r.at[1]).start()
    extra[...] = dot_nt(kd_dlogit, router[...]) + dot_nt(gate_dlogit, router[...])
    combine(0)
    combine(3)
    combine(1)
    arrived(rz, rg_r.at[1])
    s2[...] = jnp.sum(rz[...].astype(F32), axis=0)

    def to_owner(s, _):
        dx, dy, _ = offsets(s)
        tx, ty = (x + dx) % 4, (y + dy) % 4
        remote(s2.at[tx * 4 + ty], rx.at[x * 4 + y], rg_s.at[2], rg_r.at[2], ident(tx, ty, z, k)).start()
        return 0

    lax.fori_loop(1, 16, to_owner, 0)
    pltpu.make_async_copy(s2.at[x * 4 + y], rx.at[x * 4 + y], rg_r.at[2]).start()
    combine(4)
    combine(2)
    combine(5)
    arrived(rx, rg_r.at[2])
    router_grad[...] = jnp.sum(rx[...], axis=0)[:28, :] / math.sqrt(E * T)

    for i in (0, 3, 1, 4, 2, 5):
        wide = RETURN[i][1]
        arrived(back[i], part_r.at[i])
        for q in range(2):
            cols = slice(RBASE[i] + q * wide, RBASE[i] + (q + 1) * wide)
            token_grad[:, cols] = (jnp.sum(back[i][q].astype(F32), axis=0) + extra[:, cols]).astype(BF)

    for i in range(NC):
        arrived(r1[i].at[:, pl.ds(0, 7)], r1_s.at[i])
        arrived(x2[i].at[0], x2_s.at[i])
        arrived(x2[i].at[0, pl.ds(0, 15)], x2_s.at[i])
    for i in range(NR):
        arrived(yin[i].at[pl.ds(0, 31)], y_s.at[i])
        arrived(part[i].at[pl.ds(0, 7)], part_s.at[i])
    for axis in range(3):
        arrived(meta_in.at[axis, pl.ds(0, 7)], meta_s.at[axis])
    arrived(pg_in.at[pl.ds(0, 15)], pg_s)
    arrived(bp_in.at[pl.ds(0, 7)], bp_s)
    to_core.wait_send()
    arrived(rz.at[pl.ds(0, 3)], rg_s.at[1])
    arrived(rx.at[pl.ds(0, 15)], rg_s.at[2])


def local(tokens, cotangent, router, picks, language, teacher, w_gate, w_up, w_down):
    vmem, anywhere = pl.BlockSpec(memory_space=pltpu.VMEM), pl.BlockSpec(memory_space=pl.ANY)
    buf, sem = pltpu.VMEM, pltpu.SemaphoreType.DMA
    per = lambda make, chunks=CHUNKS: tuple(buf(make(wide), BF) for _, wide in chunks)
    scratch = [
        buf((D, FF), BF), buf((D, FF), BF), buf((FF, D), BF),
        buf((2, T, D), BF),
        buf((12, T, 128), BF), buf((3, 8, T, 128), BF),
        buf((3, 768, 256), BF), buf((3, 256, 768), BF),
        per(lambda c: (2, 8, T, c)),
        per(lambda c: (32, 48, c)), per(lambda c: (2, 16, 48, c)),
        buf((ROWS, D), BF), buf((16, 24, D), BF),
        buf((3, ROWS, FF), F32), buf((ROWS, 2 * FF), BF),
        per(lambda c: (32, 24, c), RETURN),
        per(lambda c: (8, T, c), RETURN), per(lambda c: (2, 4, T, c), RETURN),
        buf((16, 24, 128), BF), buf((16, 24, 128), BF),
        buf((8, T, 128), BF), buf((8, T, 128), BF),
        buf((3, T, E), F32), buf((T, D), F32),
        buf((904, 128), F32), buf((2, 64, 32, 128), BF), buf((64, 32, 128), BF),
        buf((64, 32, 128), BF), buf((4, 16, 32, 128), BF),
        buf((16, 32, 128), F32), buf((16, 32, 128), F32),
        pltpu.SemaphoreType.REGULAR, sem((3,)), sem((3,)),
        sem((NC,)), sem((NC,)), sem((3,)), sem((3,)), sem((NC,)), sem((NC,)), sem((NR,)), sem((NR,)), sem((NR,)), sem((NR,)),
        sem, sem, sem, sem, sem((3,)), sem((3,)),
    ]
    return pl.pallas_call(
        kernel,
        out_shape=(jax.ShapeDtypeStruct((T, D), BF), jax.ShapeDtypeStruct((28, 128), F32)),
        in_specs=[anywhere, anywhere, vmem, vmem, vmem, vmem, anywhere, anywhere, anywhere, vmem, anywhere]
        + [vmem] * 5,
        out_specs=(vmem, vmem),
        scratch_shapes=scratch,
        compiler_params=pltpu.CompilerParams(
            collective_id=0, has_side_effects=True, vmem_limit_bytes=61 << 20
        ),
        cost_estimate=pl.CostEstimate(flops=15_000_000_000, bytes_accessed=24_000_000, transcendentals=400_000),
    )(tokens, cotangent, router, picks.T, language.reshape(1, T), teacher, w_gate, w_up, w_down, *tables())


def solution(mesh):
    split = P(("row", "col"), None)
    cube = P(("row", "col"), None, None)
    return jax.shard_map(
        local,
        mesh=mesh,
        in_specs=(split, split, P(), split, P(("row", "col")), P(), cube, cube, cube),
        out_specs=(split, split),
        check_vma=False,
    )
```

time: 149 us -> 124 us (0.83)
  Pallas kernels: 142 us -> 120 us
  local copies, waits for them, and re-layouts: 5.67 us -> 2.96 us
    pallas_call x1, Pallas kernels: 142 us -> 120 us  [local(): pl.pallas_call(kernel, out_shape=(jax.ShapeDtypeStruct((T, D), BF), jax.S...]
    unnamed x3 -> x2, local copies, waits for them, and re-layouts: 4.33 us -> 2.96 us
where the time goes in v2:
time: 124 us
  Pallas kernels  120 us (97%)
  local copies, waits for them, and re-layouts  2.96 us (2%)
    pallas_call x1, Pallas kernels, local(): pl.pallas_call(kernel, out_shape=(jax.ShapeDtypeStruct((T, D), BF), jax.S...  120 us
    unnamed x2, local copies, waits for them, and re-layouts  2.96 us

profile of v2, /device:TPU:1, one launch (start us, length us, event | category | flops | bytes accessed | tf_op | source)
XLA Modules:
  0.0 124.1 jit_solution(1764715750419020565)
XLA Ops:
  0.6 120.5 %shard_map.167 = (bf16[32,3584]{1,0:T(8,128)(2,1)}, f32[28,128]{1,0:T(8,128)}) custom-call(bf16[32,3584]{1,0:T(8,128)(2,1)} %tokens.1, bf16[32,3584]{1,0:T(8,128)(2,1)} %cotangent.1, bf16[3584,128]{1,0:T(8,128)(2,1)} %router.1, s32[8,32]{1,0:T(8,128)} %bitcast.2, s32[1,32]{1,0:T(1,128)} %bitcast.3, f32[8,128]{1,0:T(8,128)} %teacher.1, ...), custom_call_target="tpu_custom_call" | custom-call | flops 15000000512 | bytes 24000000 | tf_op jit(solution)/shard_map/pallas_call | solution.py:479
  121.1 1.6 %copy.20 = bf16[32,3584]{1,0:T(8,128)(2,1)} copy(bf16[32,3584]{1,0:T(8,128)(2,1)} %get-tuple-element.4) | data formatting | bytes 458752
  122.8 1.3 %copy.21 = f32[28,128]{1,0:T(8,128)} copy(f32[28,128]{1,0:T(8,128)} %get-tuple-element.5) | data formatting | bytes 28672

commit v3 on v2

--- a/solution.py
+++ b/solution.py
@@ -16,7 +16,7 @@
 SETS = ((0, 1, 2), (3, 4, 5), (6, 7, 8))
 BASE = tuple(sum(2 * c for _, c in CHUNKS[:i]) for i in range(len(CHUNKS)))
 NC = len(CHUNKS)
-RETURN = ((0, 512), (1, 512), (2, 384), (0, 128), (1, 128), (2, 128))
+RETURN = ((0, 128), (1, 128), (2, 128), (0, 256), (1, 256), (2, 256), (0, 256), (1, 256), (2, 128))
 RBASE = tuple(sum(2 * c for _, c in RETURN[:i]) for i in range(len(RETURN)))
 NR = len(RETURN)
 ROWS = 384
@@ -59,10 +59,8 @@
     spread = np.stack([row // 24 == lane, row // 24 + 32 == lane]).astype(np.float32)
     own, col = row % 24 // 3, np.arange(256)[None, :] // 32
     slot = np.where(own == col, row % 3 + 1, 9).astype(np.float32)
-    short = np.arange(ROWS)[:, None]
-    half = np.stack([short // 24 * 2 + k == lane for k in range(2)]).astype(np.float32)
     as_bf = lambda array: jnp.asarray(array, BF)
-    return (as_bf(perm), as_bf(select), as_bf(spread), as_bf(slot[:24]), as_bf(slot[:ROWS].T), as_bf(half), as_bf(eye))
+    return (as_bf(perm), as_bf(select), as_bf(spread), as_bf(slot[:24]), as_bf(slot[:ROWS].T), as_bf(eye))
 
 
 def dot(a, b):
@@ -83,10 +81,10 @@
 
 def kernel(
     tokens, cotangent, router, picks, language, teacher, w_gate, w_up, w_down,
-    perm, select_hbm, spread, slot, slot_t, half, eye,
+    perm, select_hbm, spread, slot, slot_t, eye,
     token_grad, router_grad,
     wg, wu, wd, rows, meta_out, meta_in, pick_l, mix_w, r1, out2, x2, xt, xc, acc, grads,
-    yin, part, back, pg_out, pg_in, bp_out, bp_in, route, extra, rgs, rgb, rk, s1, rz, s2, rx,
+    yin, part, back, pg_out, pg_in, bp_out, bp_in, route, rgs, rgb, rk, s1, rz, rx,
     ready, w_sem, in_sem, r1_s, r1_r, meta_s, meta_r, x2_s, x2_r, y_s, y_r, part_s, part_r, pg_s, pg_r, bp_s, bp_r, rg_s, rg_r,
 ):
     me_row, me_col = lax.axis_index("row"), lax.axis_index("col")
@@ -160,38 +158,41 @@
     pl.semaphore_wait(barrier, 19)
     greet(ready)
 
-    for axis in range(3):
-        u, v, w = places[axis]
-        mine = u * 2 + k
-
-        def tell(s, _, axis=axis, u=u, v=v, w=w, mine=mine):
-            to = (u + s // 2) % 4
-            core = (k + s) % 2
+    def tell(s, _):
+        for axis in range(3):
+            u, v, w = places[axis]
+            to, core = (u + s // 2) % 4, (k + s) % 2
             remote(
-                meta_out.at[axis * 4 + to], meta_in.at[axis, mine], meta_s.at[axis], meta_r.at[axis],
+                meta_out.at[axis * 4 + to], meta_in.at[axis, u * 2 + k], meta_s.at[axis], meta_r.at[axis],
                 device(axis, to, v, w, core),
             ).start()
+        return 0
+
+    lax.fori_loop(1, 8, tell, 0)
+    for axis in range(3):
+        u = places[axis][0]
+        pltpu.make_async_copy(meta_out.at[axis * 4 + u], meta_in.at[axis, u * 2 + k], meta_r.at[axis]).start()
+
+    for chunks in SETS:
+
+        def hop(s, _, chunks=chunks):
+            for i in chunks:
+                axis, wide = CHUNKS[i]
+                u, v, w = places[axis]
+                core = (k + s) % 2
+                start = pl.multiple_of(BASE[i] + core * wide, 128)
+                remote(
+                    rows.at[:, :, pl.ds(start, wide)], r1[i].at[:, u * 2 + k], r1_s.at[i], r1_r.at[i],
+                    device(axis, (u + s // 2) % 4, v, w, core),
+                ).start()
             return 0
 
-        lax.fori_loop(1, 8, tell, 0)
-        pltpu.make_async_copy(meta_out.at[axis * 4 + u], meta_in.at[axis, mine], meta_r.at[axis]).start()
-
-    for i, (axis, wide) in enumerate(CHUNKS):
-        u, v, w = places[axis]
-        mine = u * 2 + k
-
-        def hop(s, _, i=i, axis=axis, wide=wide, u=u, v=v, w=w, mine=mine):
-            du, core = s // 2, (k + s) % 2
-            start = pl.multiple_of(BASE[i] + core * wide, 128)
-            remote(
-                rows.at[:, :, pl.ds(start, wide)], r1[i].at[:, mine], r1_s.at[i], r1_r.at[i],
-                device(axis, (u + du) % 4, v, w, core),
-            ).start()
-            return 0
-
         lax.fori_loop(1, 8, hop, 0)
-        start = pl.multiple_of(BASE[i] + k * wide, 128)
-        pltpu.make_async_copy(rows.at[:, :, pl.ds(start, wide)], r1[i].at[:, mine], r1_r.at[i]).start()
+        for i in chunks:
+            axis, wide = CHUNKS[i]
+            start = pl.multiple_of(BASE[i] + k * wide, 128)
+            into = r1[i].at[:, places[axis][0] * 2 + k]
+            pltpu.make_async_copy(rows.at[:, :, pl.ds(start, wide)], into, r1_r.at[i]).start()
 
     def offsets(s):
         j = s % 16
@@ -302,38 +303,41 @@
 
     def permute(axis):
         if axis:
-            xt[:, 0 : 2 * FF] = dot_tn(perm[axis - 1], grads[...]).astype(BF)
+            xt[:, (axis - 1) * 2 * FF : axis * 2 * FF] = dot_tn(perm[axis - 1], grads[...]).astype(BF)
 
     def produce(i, dq):
         axis, wide = RETURN[i]
         cols = pl.ds(pl.multiple_of(RBASE[i] + (k + dq) % 2 * wide, 128), wide)
-        lhs = xt if axis else grads
-        got = dot_nt(lhs[:, :FF], wg[cols, :]) + dot_nt(lhs[:, FF : 2 * FF], wu[cols, :])
+        lhs = xt.at[:, (axis - 1) * 2 * FF : axis * 2 * FF] if axis else grads
+        got = dot_nt(lhs[:, :FF], wg[cols, :]) + dot_nt(lhs[:, FF:], wu[cols, :])
         xc[:, :, cols] = got.astype(BF).reshape(16, 24, wide)
 
-    def give(i, dq):
-        axis, wide = RETURN[i]
-        u, v, w = places[axis]
-        q = (k + dq) % 2
-        cols = pl.ds(pl.multiple_of(RBASE[i] + q * wide, 128), wide)
-
+    def give(chunks):
         def one(s, _):
-            dv, dw, _ = offsets(s)
-            tv, tw = (v + dv) % 4, (w + dw) % 4
-            remote(
-                xc.at[tv * 4 + tw, :, cols], yin[i].at[v * 8 + w * 2 + k], y_s.at[i], y_r.at[i],
-                device(axis, u, tv, tw, q),
-            ).start()
+            dv, dw, dk = offsets(s)
+            for i in chunks:
+                axis, wide = RETURN[i]
+                u, v, w = places[axis]
+                tv, tw, q = (v + dv) % 4, (w + dw) % 4, (k + dk) % 2
+                cols = pl.ds(pl.multiple_of(RBASE[i] + q * wide, 128), wide)
+                remote(
+                    xc.at[tv * 4 + tw, :, cols], yin[i].at[v * 8 + w * 2 + k], y_s.at[i], y_r.at[i],
+                    device(axis, u, tv, tw, q),
+                ).start()
             return 0
 
-        lax.fori_loop(1 - dq, 16, one, 0)
-        if dq == 0:
+        lax.fori_loop(1, 32, one, 0)
+        for i in chunks:
+            axis, wide = RETURN[i]
+            u, v, w = places[axis]
+            cols = pl.ds(pl.multiple_of(RBASE[i] + k * wide, 128), wide)
             pltpu.make_async_copy(xc.at[v * 4 + w, :, cols], yin[i].at[v * 8 + w * 2 + k], y_r.at[i]).start()
 
-    def whole(i):
-        for dq in range(2):
-            produce(i, dq)
-            give(i, dq)
+    def extra(start, wide):
+        return acc.at[0, start // FF * T : start // FF * T + T, start % FF : start % FF + wide]
+
+    def share(i):
+        return acc.at[1, pl.ds(pl.multiple_of(i // 8 * 32, 32), 32), pl.ds(pl.multiple_of(i % 8 * 128, 128), 128)]
 
     def combine(i):
         axis, wide = RETURN[i]
@@ -351,19 +355,19 @@
         lax.fori_loop(1, 8, give_back, 0)
         pltpu.make_async_copy(part[i].at[u * 2 + k], back[i].at[k, u], part_r.at[i]).start()
 
-    produce(0, 0)
-    give(0, 0)
-    produce(0, 1)
-    give(0, 1)
+    for axis in range(2):
+        permute(axis)
+        for dq in range(2):
+            produce(axis, dq)
+        give((axis,))
 
     arrived(pg_in, pg_r)
     codes = meta_in[0].reshape(256, 128)
-    wanted = jnp.where(dot_nt(codes, half[k]) == slot_t[...].astype(F32), 1.0, 0.0).astype(BF)
-    line = lax.broadcasted_iota(jnp.int32, (ROWS, 128), 0)
-    owner = 32 * z + 2 * ((line * 2731) >> 16) + k
-    values = jnp.where(
-        lax.broadcasted_iota(jnp.int32, (ROWS, 128), 1) == owner, pg_in[...].reshape(ROWS, 128).astype(F32), 0.0
-    ).astype(BF)
+    line, lane = (lax.broadcasted_iota(jnp.int32, (ROWS, 128), dim) for dim in (0, 1))
+    owner = 2 * ((line * 2731) >> 16) + k
+    one_of = jnp.where(lane == owner, 1.0, 0.0).astype(BF)
+    wanted = jnp.where(dot_nt(codes, one_of) == slot_t[...].astype(F32), 1.0, 0.0).astype(BF)
+    values = jnp.where(lane == 32 * z + owner, pg_in[...].reshape(ROWS, 128).astype(F32), 0.0).astype(BF)
     bp_out[...] = dot(wanted, values).astype(BF).reshape(8, T, 128)
 
     def send_dense(s, _):
@@ -374,10 +378,14 @@
     lax.fori_loop(1, 8, send_dense, 0)
     pltpu.make_async_copy(bp_out.at[z * 2 + k], bp_in.at[z * 2 + k], bp_r).start()
 
-    whole(3)
-    permute(1)
-    whole(1)
-    whole(4)
+    permute(2)
+    for dq in range(2):
+        produce(2, dq)
+    give((2,))
+    for i in SETS[1]:
+        for dq in range(2):
+            produce(i, dq)
+    give(SETS[1])
 
     arrived(bp_in, bp_r)
     pick_back = jnp.sum(bp_in[...].astype(F32), axis=0)
@@ -394,9 +402,9 @@
     to_core = remote(rgb.at[1 - k], rk, rg_s.at[0], rg_r.at[0], ident(x, y, z, 1 - k))
     to_core.start()
 
-    permute(2)
-    whole(2)
-    whole(5)
+    for i in SETS[2]:
+        for dq in range(2):
+            produce(i, dq)
     to_core.wait_recv()
     s1[...] = (rgb[k].astype(F32) + rk[...].astype(F32)).astype(BF)
 
@@ -407,33 +415,36 @@
 
     lax.fori_loop(1, 4, to_plane, 0)
     pltpu.make_async_copy(s1.at[pl.ds(z * 16, 16)], rz.at[z], rg_r.at[1]).start()
-    extra[...] = dot_nt(kd_dlogit, router[...]) + dot_nt(gate_dlogit, router[...])
-    combine(0)
-    combine(3)
-    combine(1)
+    give(SETS[2])
+    for j in range(7):
+        cols = slice(j * 512, j * 512 + 512)
+        extra(j * 512, 512)[...] = dot_nt(kd_dlogit, router[cols, :]) + dot_nt(gate_dlogit, router[cols, :])
+    for i in SETS[0] + SETS[1]:
+        combine(i)
     arrived(rz, rg_r.at[1])
-    s2[...] = jnp.sum(rz[...].astype(F32), axis=0)
+    for i in range(16):
+        share(i)[...] = jnp.sum(rz[:, i].astype(F32), axis=0)
 
     def to_owner(s, _):
         dx, dy, _ = offsets(s)
         tx, ty = (x + dx) % 4, (y + dy) % 4
-        remote(s2.at[tx * 4 + ty], rx.at[x * 4 + y], rg_s.at[2], rg_r.at[2], ident(tx, ty, z, k)).start()
+        remote(share(tx * 4 + ty), rx.at[x * 4 + y], rg_s.at[2], rg_r.at[2], ident(tx, ty, z, k)).start()
         return 0
 
     lax.fori_loop(1, 16, to_owner, 0)
-    pltpu.make_async_copy(s2.at[x * 4 + y], rx.at[x * 4 + y], rg_r.at[2]).start()
-    combine(4)
-    combine(2)
-    combine(5)
+    pltpu.make_async_copy(share(x * 4 + y), rx.at[x * 4 + y], rg_r.at[2]).start()
+    for i in SETS[2]:
+        combine(i)
     arrived(rx, rg_r.at[2])
     router_grad[...] = jnp.sum(rx[...], axis=0)[:28, :] / math.sqrt(E * T)
 
-    for i in (0, 3, 1, 4, 2, 5):
+    for i in range(NR):
         wide = RETURN[i][1]
         arrived(back[i], part_r.at[i])
         for q in range(2):
-            cols = slice(RBASE[i] + q * wide, RBASE[i] + (q + 1) * wide)
-            token_grad[:, cols] = (jnp.sum(back[i][q].astype(F32), axis=0) + extra[:, cols]).astype(BF)
+            start = RBASE[i] + q * wide
+            total = jnp.sum(back[i][q].astype(F32), axis=0) + extra(start, wide)[...]
+            token_grad[:, start : start + wide] = total.astype(BF)
 
     for i in range(NC):
         arrived(r1[i].at[:, pl.ds(0, 7)], r1_s.at[i])
@@ -462,16 +473,16 @@
         buf((3, 768, 256), BF), buf((3, 256, 768), BF),
         per(lambda c: (2, 8, T, c)),
         per(lambda c: (32, 48, c)), per(lambda c: (2, 16, 48, c)),
-        buf((ROWS, D), BF), buf((16, 24, D), BF),
+        buf((ROWS, 4 * FF), BF), buf((16, 24, D), BF),
         buf((3, ROWS, FF), F32), buf((ROWS, 2 * FF), BF),
         per(lambda c: (32, 24, c), RETURN),
         per(lambda c: (8, T, c), RETURN), per(lambda c: (2, 4, T, c), RETURN),
         buf((16, 24, 128), BF), buf((16, 24, 128), BF),
         buf((8, T, 128), BF), buf((8, T, 128), BF),
-        buf((3, T, E), F32), buf((T, D), F32),
+        buf((3, T, E), F32),
         buf((904, 128), F32), buf((2, 64, 32, 128), BF), buf((64, 32, 128), BF),
         buf((64, 32, 128), BF), buf((4, 16, 32, 128), BF),
-        buf((16, 32, 128), F32), buf((16, 32, 128), F32),
+        buf((16, 32, 128), F32),
         pltpu.SemaphoreType.REGULAR, sem((3,)), sem((3,)),
         sem((NC,)), sem((NC,)), sem((3,)), sem((3,)), sem((NC,)), sem((NC,)), sem((NR,)), sem((NR,)), sem((NR,)), sem((NR,)),
         sem, sem, sem, sem, sem((3,)), sem((3,)),
@@ -480,7 +491,7 @@
         kernel,
         out_shape=(jax.ShapeDtypeStruct((T, D), BF), jax.ShapeDtypeStruct((28, 128), F32)),
         in_specs=[anywhere, anywhere, vmem, vmem, vmem, vmem, anywhere, anywhere, anywhere, vmem, anywhere]
-        + [vmem] * 5,
+        + [vmem] * 4,
         out_specs=(vmem, vmem),
         scratch_shapes=scratch,
         compiler_params=pltpu.CompilerParams(

time: 124 us -> 119 us (0.960)
  Pallas kernels: 120 us -> 115 us
    pallas_call x1, Pallas kernels: 120 us -> 115 us  [local(): pl.pallas_call(kernel, out_shape=(jax.ShapeDtypeStruct((T, D), BF), jax.S...]
where the time goes in v3:
time: 119 us
  Pallas kernels  115 us (97%)
  local copies, waits for them, and re-layouts  2.96 us (2%)
    pallas_call x1, Pallas kernels, local(): pl.pallas_call(kernel, out_shape=(jax.ShapeDtypeStruct((T, D), BF), jax.S...  115 us
    unnamed x2, local copies, waits for them, and re-layouts  2.96 us

profile of v3, /device:TPU:1, one launch (start us, length us, event | category | flops | bytes accessed | tf_op | source)
XLA Modules:
  0.0 118.9 jit_solution(3232313188805896259)
XLA Ops:
  0.6 115.3 %shard_map.158 = (bf16[32,3584]{1,0:T(8,128)(2,1)}, f32[28,128]{1,0:T(8,128)}) custom-call(bf16[32,3584]{1,0:T(8,128)(2,1)} %tokens.1, bf16[32,3584]{1,0:T(8,128)(2,1)} %cotangent.1, bf16[3584,128]{1,0:T(8,128)(2,1)} %router.1, s32[8,32]{1,0:T(8,128)} %bitcast.2, s32[1,32]{1,0:T(1,128)} %bitcast.3, f32[8,128]{1,0:T(8,128)} %teacher.1, ...), custom_call_target="tpu_custom_call" | custom-call | flops 15000000512 | bytes 24000000 | tf_op jit(solution)/shard_map/pallas_call | solution.py:490
  116.0 1.6 %copy.19 = bf16[32,3584]{1,0:T(8,128)(2,1)} copy(bf16[32,3584]{1,0:T(8,128)(2,1)} %get-tuple-element.4) | data formatting | bytes 458752
  117.6 1.3 %copy.20 = f32[28,128]{1,0:T(8,128)} copy(f32[28,128]{1,0:T(8,128)} %get-tuple-element.5) | data formatting | bytes 28672

commit v4 on v3

--- a/solution.py
+++ b/solution.py
@@ -12,11 +12,13 @@
 ROUTE_SCALE = 2.5
 MESH = pl.DeviceIdType.MESH
 BF, F32 = jnp.bfloat16, jnp.float32
-CHUNKS = ((0, 128), (1, 128), (2, 128), (0, 384), (1, 384), (2, 256), (0, 128), (1, 128), (2, 128))
-SETS = ((0, 1, 2), (3, 4, 5), (6, 7, 8))
+Z, Y, X = (0, 0), (1, 1), (2, 2)
+CHUNKS = ((Z, 128), (Y, 128), (X, 128), (Z, 384), (Y, 256), (X, 256), ((1, 2), 128), (Z, 128), (Y, 128), (X, 128))
+SETS = ((0, 1, 2), (3, 4, 5, 6), (7, 8, 9))
 BASE = tuple(sum(2 * c for _, c in CHUNKS[:i]) for i in range(len(CHUNKS)))
 NC = len(CHUNKS)
-RETURN = ((0, 128), (1, 128), (2, 128), (0, 256), (1, 256), (2, 256), (0, 256), (1, 256), (2, 128))
+RETURN = ((Z, 128), (Y, 128), (X, 128), (Z, 256), (Y, 256), (X, 256), (Z, 256), (Y, 128), (X, 128), (Z, 128))
+RSETS = ((0, 1, 2), (3, 4, 5), (6, 7, 8, 9))
 RBASE = tuple(sum(2 * c for _, c in RETURN[:i]) for i in range(len(RETURN)))
 NR = len(RETURN)
 ROWS = 384
@@ -85,14 +87,28 @@
     token_grad, router_grad,
     wg, wu, wd, rows, meta_out, meta_in, pick_l, mix_w, r1, out2, x2, xt, xc, acc, grads,
     yin, part, back, pg_out, pg_in, bp_out, bp_in, route, rgs, rgb, rk, s1, rz, rx,
-    ready, w_sem, in_sem, r1_s, r1_r, meta_s, meta_r, x2_s, x2_r, y_s, y_r, part_s, part_r, pg_s, pg_r, bp_s, bp_r, rg_s, rg_r,
+    ready, w_sem, in_sem, r1_s, r1_r, meta_s, meta_r, share_s, share_r, x2_s, x2_r, y_s, y_r, part_s, part_r, pg_s, pg_r, bp_s, bp_r, rg_s, rg_r,
 ):
     me_row, me_col = lax.axis_index("row"), lax.axis_index("col")
     x, y, z, k = (me_row % 2) * 2 + me_col // 8, (me_col // 2) % 4, me_row // 2, me_col % 2
     places = [uvw_of(axis, x, y, z) for axis in range(3)]
 
-    def device(axis, u, v, w, core):
-        return ident(*xyz_of(axis, u, v, w), core)
+    def by_core(values, core):
+        return values[0] + core * (values[1] - values[0])
+
+    def spot(axes, relay):
+        if axes[0] == axes[1]:
+            return places[axes[0]]
+        return tuple(by_core(pair, relay) for pair in zip(places[axes[0]], places[axes[1]]))
+
+    def device(axes, relay, u, v, w, core):
+        first, second = (xyz_of(axis, u, v, w) for axis in axes)
+        if axes[0] == axes[1]:
+            return ident(*first, core)
+        return ident(*(by_core(pair, relay) for pair in zip(first, second)), core)
+
+    def axis_of(axes, relay):
+        return axes[0] if axes[0] == axes[1] else by_core(axes, relay)
 
     def remote(src, dst, send, recv, where):
         return pltpu.make_async_remote_copy(
@@ -120,7 +136,7 @@
             u, v, w = places[axis]
 
             def one(s, _, axis=axis, u=u, v=v, w=w):
-                where = device(axis, (u + s // 2) % 4, v, w, (k + s) % 2)
+                where = device((axis, axis), 0, (u + s // 2) % 4, v, w, (k + s) % 2)
                 pl.semaphore_signal(sem, inc=1, device_id=where, device_id_type=MESH)
                 return 0
 
@@ -136,6 +152,10 @@
     rank = dot(asked.astype(BF), jnp.where(before, 1.0, 0.0).astype(BF))
     code = dot_tn((asked * (rank + 1.0)).astype(BF), eye[...])
     picked = jnp.where(code > 0.0, 1.0, 0.0)
+    inputs[2].wait()
+    told = dot(code.astype(BF), select[0:E, :])
+    for m in range(12):
+        meta_out[m] = told[:, m * 128 : (m + 1) * 128].astype(BF)
     spoken = jnp.where(lax.broadcasted_iota(jnp.int32, (LANGS, T), 0) == language[...], 1.0, 0.0).astype(BF)
     target, left = jnp.zeros((T, E), F32), teacher[...]
     for _ in range(3):
@@ -143,8 +163,53 @@
         left = left - piece.astype(F32)
         target += dot_tn(spoken, piece)
 
-    for copy in inputs:
+    pl.semaphore_wait(barrier, 19)
+    greet(ready)
+
+    def tell(source, into, send, recv):
+        def one(s, _):
+            for axis in range(3):
+                u, v, w = places[axis]
+                to, core = (u + s // 2) % 4, (k + s) % 2
+                remote(
+                    source.at[axis * 4 + to], into.at[axis * 8 + u * 2 + k], send.at[axis], recv.at[axis],
+                    device((axis, axis), 0, to, v, w, core),
+                ).start()
+            return 0
+
+        lax.fori_loop(1, 8, one, 0)
+        for axis in range(3):
+            u = places[axis][0]
+            pltpu.make_async_copy(source.at[axis * 4 + u], into.at[axis * 8 + u * 2 + k], recv.at[axis]).start()
+
+    share_out, share_in = rgb.at[0], rk
+
+    def send_rows(chunks):
+        def hop(s, _):
+            core = (k + s) % 2
+            for i in chunks:
+                axes, wide = CHUNKS[i]
+                u, v, w = spot(axes, core)
+                start = pl.multiple_of(BASE[i] + core * wide, 128)
+                remote(
+                    rows.at[:, :, pl.ds(start, wide)], r1[i].at[:, u * 2 + k], r1_s.at[i], r1_r.at[i],
+                    device(axes, core, (u + s // 2) % 4, v, w, core),
+                ).start()
+            return 0
+
+        lax.fori_loop(1, 8, hop, 0)
+        for i in chunks:
+            axes, wide = CHUNKS[i]
+            start = pl.multiple_of(BASE[i] + k * wide, 128)
+            into = r1[i].at[:, spot(axes, k)[0] * 2 + k]
+            pltpu.make_async_copy(rows.at[:, :, pl.ds(start, wide)], into, r1_r.at[i]).start()
+
+    tell(meta_out, meta_in, meta_s, meta_r)
+    for copy in inputs[:2]:
         copy.wait()
+    for chunks in SETS:
+        send_rows(chunks)
+
     logits = dot(rows[0], router[...])
     scores = jax.nn.sigmoid(logits)
     chosen = picked * scores
@@ -152,65 +217,29 @@
     route[0] = weight
     route[1] = weight * (1.0 - scores)
     route[2] = scores - target
-    told = dot(code.astype(BF), select[0:E, :]) + dot(weight.astype(BF), select[E:, :])
+    told = dot(weight.astype(BF), select[E:, :])
     for m in range(12):
-        meta_out[m] = told[:, m * 128 : (m + 1) * 128].astype(BF)
-    pl.semaphore_wait(barrier, 19)
-    greet(ready)
-
-    def tell(s, _):
-        for axis in range(3):
-            u, v, w = places[axis]
-            to, core = (u + s // 2) % 4, (k + s) % 2
-            remote(
-                meta_out.at[axis * 4 + to], meta_in.at[axis, u * 2 + k], meta_s.at[axis], meta_r.at[axis],
-                device(axis, to, v, w, core),
-            ).start()
-        return 0
-
-    lax.fori_loop(1, 8, tell, 0)
-    for axis in range(3):
-        u = places[axis][0]
-        pltpu.make_async_copy(meta_out.at[axis * 4 + u], meta_in.at[axis, u * 2 + k], meta_r.at[axis]).start()
-
-    for chunks in SETS:
-
-        def hop(s, _, chunks=chunks):
-            for i in chunks:
-                axis, wide = CHUNKS[i]
-                u, v, w = places[axis]
-                core = (k + s) % 2
-                start = pl.multiple_of(BASE[i] + core * wide, 128)
-                remote(
-                    rows.at[:, :, pl.ds(start, wide)], r1[i].at[:, u * 2 + k], r1_s.at[i], r1_r.at[i],
-                    device(axis, (u + s // 2) % 4, v, w, core),
-                ).start()
-            return 0
-
-        lax.fori_loop(1, 8, hop, 0)
-        for i in chunks:
-            axis, wide = CHUNKS[i]
-            start = pl.multiple_of(BASE[i] + k * wide, 128)
-            into = r1[i].at[:, places[axis][0] * 2 + k]
-            pltpu.make_async_copy(rows.at[:, :, pl.ds(start, wide)], into, r1_r.at[i]).start()
+        share_out.at[m][...] = told[:, m * 128 : (m + 1) * 128].astype(BF)
+
+    tell(share_out, share_in, share_s, share_r)
 
     def offsets(s):
         j = s % 16
         return j % 4, (j // 4 + j) % 4, s // 16
 
     for axis in range(3):
-        arrived(meta_in.at[axis], meta_r.at[axis])
-        codes = meta_in[axis].reshape(256, 128)
+        arrived(meta_in.at[axis * 8 : axis * 8 + 8], meta_r.at[axis])
+        codes = meta_in[axis * 8 : axis * 8 + 8].reshape(256, 128)
         slots = jnp.broadcast_to(slot[...].astype(F32)[None], (32, 24, 256)).reshape(768, 256)
         pick_l[axis] = jnp.where(dot_nt(spread[0], codes) == slots, 1.0, 0.0).astype(BF)
 
     def relay(chunks):
         for i in chunks:
-            axis, wide = CHUNKS[i]
+            axes, wide = CHUNKS[i]
             arrived(r1[i], r1_r.at[i])
 
-            def gather(g, _, i=i, axis=axis, wide=wide):
-                lhs = pick_l[axis, pl.ds(pl.multiple_of(g * 192, 192), 192), :]
+            def gather(g, _, i=i, axes=axes, wide=wide):
+                lhs = pick_l[axis_of(axes, k), pl.ds(pl.multiple_of(g * 192, 192), 192), :]
                 for a in range(2):
                     got = dot(lhs, r1[i][a].reshape(256, wide)).astype(BF)
                     out2[i][pl.ds(g * 8, 8), a * 24 : a * 24 + 24, :] = got.reshape(8, 24, wide)
@@ -224,18 +253,18 @@
         def spread_out(s, _):
             dv, dw, dk = offsets(s)
             for i in chunks:
-                axis, wide = CHUNKS[i]
-                u, v, w = places[axis]
+                axes, wide = CHUNKS[i]
+                u, v, w = spot(axes, k)
                 tv, tw, core = (v + dv) % 4, (w + dw) % 4, (k + dk) % 2
                 remote(
                     out2[i].at[tv * 8 + tw * 2 + core], x2[i].at[k, v * 4 + w], x2_s.at[i], x2_r.at[i],
-                    device(axis, u, tv, tw, core),
+                    device(axes, k, u, tv, tw, core),
                 ).start()
             return 0
 
         lax.fori_loop(1, 32, spread_out, 0)
         for i in chunks:
-            u, v, w = places[CHUNKS[i][0]]
+            u, v, w = spot(CHUNKS[i][0], k)
             pltpu.make_async_copy(out2[i].at[v * 8 + w * 2 + k], x2[i].at[k, v * 4 + w], x2_r.at[i]).start()
 
     for chunks in SETS:
@@ -243,18 +272,25 @@
 
     slots_t = jnp.concatenate([slot_t[...].astype(F32)] * 2, axis=1)
     for axis in range(3):
-        codes = meta_in[axis].reshape(256, 128)
-        mix_w[axis] = jnp.where(dot_nt(codes, spread[0]) == slots_t, dot_nt(codes, spread[1]), 0.0).astype(BF)
+        arrived(share_in.at[axis * 8 : axis * 8 + 8], share_r.at[axis])
+        codes, shares = (ref[axis * 8 : axis * 8 + 8].reshape(256, 128) for ref in (meta_in, share_in))
+        mix_w[axis] = jnp.where(dot_nt(codes, spread[0]) == slots_t, dot_nt(shares, spread[1]), 0.0).astype(BF)
 
     def collect(chunks):
         for i in chunks:
-            axis, wide = CHUNKS[i]
+            axes, wide = CHUNKS[i]
             arrived(x2[i], x2_r.at[i])
-            for q in range(2):
-                cols = slice(BASE[i] + q * wide, BASE[i] + (q + 1) * wide)
-                for a in range(2):
-                    got = x2[i][q, :, a * 24 : a * 24 + 24, :].reshape(ROWS, wide)
-                    got = got if axis == 0 else dot(perm[axis - 1], got).astype(BF)
+            taken = [(q, a) for q in range(2) for a in range(2)]
+            every = [x2[i][q, :, a * 24 : a * 24 + 24, :].reshape(ROWS, wide) for q, a in taken]
+            step = 4 if axes[0] == axes[1] and wide == 128 else 2
+            for n in range(0, 4, step):
+                axis = axes[taken[n][0]]
+                some = every[n : n + step]
+                if axis:
+                    moved = dot(perm[axis - 1], jnp.concatenate(some, axis=1)).astype(BF)
+                    some = [moved[:, j * wide : (j + 1) * wide] for j in range(step)]
+                for (q, a), got in zip(taken[n : n + step], some):
+                    cols = slice(BASE[i] + q * wide, BASE[i] + (q + 1) * wide)
                     if a == 0:
                         xt[:, cols] = got
                     else:
@@ -306,9 +342,15 @@
             xt[:, (axis - 1) * 2 * FF : axis * 2 * FF] = dot_tn(perm[axis - 1], grads[...]).astype(BF)
 
     def produce(i, dq):
-        axis, wide = RETURN[i]
-        cols = pl.ds(pl.multiple_of(RBASE[i] + (k + dq) % 2 * wide, 128), wide)
-        lhs = xt.at[:, (axis - 1) * 2 * FF : axis * 2 * FF] if axis else grads
+        axes, wide = RETURN[i]
+        q = (k + dq) % 2
+        cols = pl.ds(pl.multiple_of(RBASE[i] + q * wide, 128), wide)
+        if axes == Z:
+            lhs = grads
+        elif axes[0] == axes[1]:
+            lhs = xt.at[:, (axes[0] - 1) * 2 * FF : axes[0] * 2 * FF]
+        else:
+            lhs = xt.at[:, pl.ds(pl.multiple_of((axis_of(axes, q) - 1) * 2 * FF, 128), 2 * FF)]
         got = dot_nt(lhs[:, :FF], wg[cols, :]) + dot_nt(lhs[:, FF:], wu[cols, :])
         xc[:, :, cols] = got.astype(BF).reshape(16, 24, wide)
 
@@ -316,39 +358,37 @@
         def one(s, _):
             dv, dw, dk = offsets(s)
             for i in chunks:
-                axis, wide = RETURN[i]
-                u, v, w = places[axis]
-                tv, tw, q = (v + dv) % 4, (w + dw) % 4, (k + dk) % 2
+                axes, wide = RETURN[i]
+                q = (k + dk) % 2
+                u, v, w = spot(axes, q)
+                tv, tw = (v + dv) % 4, (w + dw) % 4
                 cols = pl.ds(pl.multiple_of(RBASE[i] + q * wide, 128), wide)
                 remote(
                     xc.at[tv * 4 + tw, :, cols], yin[i].at[v * 8 + w * 2 + k], y_s.at[i], y_r.at[i],
-                    device(axis, u, tv, tw, q),
+                    device(axes, q, u, tv, tw, q),
                 ).start()
             return 0
 
         lax.fori_loop(1, 32, one, 0)
         for i in chunks:
-            axis, wide = RETURN[i]
-            u, v, w = places[axis]
+            axes, wide = RETURN[i]
+            u, v, w = spot(axes, k)
             cols = pl.ds(pl.multiple_of(RBASE[i] + k * wide, 128), wide)
             pltpu.make_async_copy(xc.at[v * 4 + w, :, cols], yin[i].at[v * 8 + w * 2 + k], y_r.at[i]).start()
 
     def extra(start, wide):
         return acc.at[0, start // FF * T : start // FF * T + T, start % FF : start % FF + wide]
 
-    def share(i):
-        return acc.at[1, pl.ds(pl.multiple_of(i // 8 * 32, 32), 32), pl.ds(pl.multiple_of(i % 8 * 128, 128), 128)]
-
     def combine(i):
-        axis, wide = RETURN[i]
-        u, v, w = places[axis]
+        axes, wide = RETURN[i]
+        u, v, w = spot(axes, k)
         arrived(yin[i], y_r.at[i])
-        part[i][...] = dot(mix_w[axis], yin[i][...].reshape(768, wide)).astype(BF).reshape(8, T, wide)
+        part[i][...] = dot(mix_w[axis_of(axes, k)], yin[i][...].reshape(768, wide)).astype(BF).reshape(8, T, wide)
 
         def give_back(s, _):
             to, core = (u + s // 2) % 4, (k + s) % 2
             remote(
-                part[i].at[to * 2 + core], back[i].at[k, u], part_s.at[i], part_r.at[i], device(axis, to, v, w, core)
+                part[i].at[to * 2 + core], back[i].at[k, u], part_s.at[i], part_r.at[i], device(axes, k, to, v, w, core)
             ).start()
             return 0
 
@@ -362,7 +402,7 @@
         give((axis,))
 
     arrived(pg_in, pg_r)
-    codes = meta_in[0].reshape(256, 128)
+    codes = meta_in[0:8].reshape(256, 128)
     line, lane = (lax.broadcasted_iota(jnp.int32, (ROWS, 128), dim) for dim in (0, 1))
     owner = 2 * ((line * 2731) >> 16) + k
     one_of = jnp.where(lane == owner, 1.0, 0.0).astype(BF)
@@ -382,10 +422,10 @@
     for dq in range(2):
         produce(2, dq)
     give((2,))
-    for i in SETS[1]:
+    for i in RSETS[1]:
         for dq in range(2):
             produce(i, dq)
-    give(SETS[1])
+    give(RSETS[1])
 
     arrived(bp_in, bp_r)
     pick_back = jnp.sum(bp_in[...].astype(F32), axis=0)
@@ -393,6 +433,8 @@
     gate_dlogit = (route[1] * (pick_back - mixed / ROUTE_SCALE)).astype(BF)
     kd_dlogit = route[2].astype(BF)
 
+    for axis in range(3):
+        arrived(share_in.at[0:7], share_s.at[axis])
     rgs[896:, :] = jnp.zeros((8, 128), F32)
     for zq in range(4):
         mine = rows[0, :, zq * 896 : (zq + 1) * 896]
@@ -402,7 +444,7 @@
     to_core = remote(rgb.at[1 - k], rk, rg_s.at[0], rg_r.at[0], ident(x, y, z, 1 - k))
     to_core.start()
 
-    for i in SETS[2]:
+    for i in RSETS[2]:
         for dq in range(2):
             produce(i, dq)
     to_core.wait_recv()
@@ -415,28 +457,28 @@
 
     lax.fori_loop(1, 4, to_plane, 0)
     pltpu.make_async_copy(s1.at[pl.ds(z * 16, 16)], rz.at[z], rg_r.at[1]).start()
-    give(SETS[2])
+    give(RSETS[2])
     for j in range(7):
         cols = slice(j * 512, j * 512 + 512)
         extra(j * 512, 512)[...] = dot_nt(kd_dlogit, router[cols, :]) + dot_nt(gate_dlogit, router[cols, :])
-    for i in SETS[0] + SETS[1]:
+    for i in RSETS[0] + RSETS[1]:
         combine(i)
     arrived(rz, rg_r.at[1])
-    for i in range(16):
-        share(i)[...] = jnp.sum(rz[:, i].astype(F32), axis=0)
+    arrived(rz.at[pl.ds(0, 3)], rg_s.at[1])
+    s1[0:16] = jnp.sum(rz[...].astype(F32), axis=0).astype(BF)
 
     def to_owner(s, _):
         dx, dy, _ = offsets(s)
         tx, ty = (x + dx) % 4, (y + dy) % 4
-        remote(share(tx * 4 + ty), rx.at[x * 4 + y], rg_s.at[2], rg_r.at[2], ident(tx, ty, z, k)).start()
+        remote(s1.at[tx * 4 + ty], rx.at[x * 4 + y], rg_s.at[2], rg_r.at[2], ident(tx, ty, z, k)).start()
         return 0
 
     lax.fori_loop(1, 16, to_owner, 0)
-    pltpu.make_async_copy(share(x * 4 + y), rx.at[x * 4 + y], rg_r.at[2]).start()
-    for i in SETS[2]:
+    pltpu.make_async_copy(s1.at[x * 4 + y], rx.at[x * 4 + y], rg_r.at[2]).start()
+    for i in RSETS[2]:
         combine(i)
     arrived(rx, rg_r.at[2])
-    router_grad[...] = jnp.sum(rx[...], axis=0)[:28, :] / math.sqrt(E * T)
+    router_grad[...] = jnp.sum(rx[...].astype(F32), axis=0)[:28, :] / math.sqrt(E * T)
 
     for i in range(NR):
         wide = RETURN[i][1]
@@ -454,11 +496,10 @@
         arrived(yin[i].at[pl.ds(0, 31)], y_s.at[i])
         arrived(part[i].at[pl.ds(0, 7)], part_s.at[i])
     for axis in range(3):
-        arrived(meta_in.at[axis, pl.ds(0, 7)], meta_s.at[axis])
+        arrived(meta_in.at[0:7], meta_s.at[axis])
     arrived(pg_in.at[pl.ds(0, 15)], pg_s)
     arrived(bp_in.at[pl.ds(0, 7)], bp_s)
     to_core.wait_send()
-    arrived(rz.at[pl.ds(0, 3)], rg_s.at[1])
     arrived(rx.at[pl.ds(0, 15)], rg_s.at[2])
 
 
@@ -469,7 +510,7 @@
     scratch = [
         buf((D, FF), BF), buf((D, FF), BF), buf((FF, D), BF),
         buf((2, T, D), BF),
-        buf((12, T, 128), BF), buf((3, 8, T, 128), BF),
+        buf((12, T, 128), BF), buf((24, T, 128), BF),
         buf((3, 768, 256), BF), buf((3, 256, 768), BF),
         per(lambda c: (2, 8, T, c)),
         per(lambda c: (32, 48, c)), per(lambda c: (2, 16, 48, c)),
@@ -482,9 +523,9 @@
         buf((3, T, E), F32),
         buf((904, 128), F32), buf((2, 64, 32, 128), BF), buf((64, 32, 128), BF),
         buf((64, 32, 128), BF), buf((4, 16, 32, 128), BF),
-        buf((16, 32, 128), F32),
+        buf((16, 32, 128), BF),
         pltpu.SemaphoreType.REGULAR, sem((3,)), sem((3,)),
-        sem((NC,)), sem((NC,)), sem((3,)), sem((3,)), sem((NC,)), sem((NC,)), sem((NR,)), sem((NR,)), sem((NR,)), sem((NR,)),
+        sem((NC,)), sem((NC,)), sem((3,)), sem((3,)), sem((3,)), sem((3,)), sem((NC,)), sem((NC,)), sem((NR,)), sem((NR,)), sem((NR,)), sem((NR,)),
         sem, sem, sem, sem, sem((3,)), sem((3,)),
     ]
     return pl.pallas_call(

time: 119 us -> 116 us (0.975)
  Pallas kernels: 115 us -> 112 us
    pallas_call x1, Pallas kernels: 115 us -> 112 us  [local(): pl.pallas_call(kernel, out_shape=(jax.ShapeDtypeStruct((T, D), BF), jax.S...]
where the time goes in v4:
time: 116 us
  Pallas kernels  112 us (97%)
  local copies, waits for them, and re-layouts  2.96 us (3%)
    pallas_call x1, Pallas kernels, local(): pl.pallas_call(kernel, out_shape=(jax.ShapeDtypeStruct((T, D), BF), jax.S...  112 us
    unnamed x2, local copies, waits for them, and re-layouts  2.96 us

profile of v4, /device:TPU:1, one launch (start us, length us, event | category | flops | bytes accessed | tf_op | source)
XLA Modules:
  0.0 115.6 jit_solution(16258341133793218612)
XLA Ops:
  0.6 112.0 %shard_map.158 = (bf16[32,3584]{1,0:T(8,128)(2,1)}, f32[28,128]{1,0:T(8,128)}) custom-call(bf16[32,3584]{1,0:T(8,128)(2,1)} %tokens.1, bf16[32,3584]{1,0:T(8,128)(2,1)} %cotangent.1, bf16[3584,128]{1,0:T(8,128)(2,1)} %router.1, s32[8,32]{1,0:T(8,128)} %bitcast.2, s32[1,32]{1,0:T(1,128)} %bitcast.3, f32[8,128]{1,0:T(8,128)} %teacher.1, ...), custom_call_target="tpu_custom_call" | custom-call | flops 15000000512 | bytes 24000000 | tf_op jit(solution)/shard_map/pallas_call | solution.py:531
  112.7 1.6 %copy.19 = bf16[32,3584]{1,0:T(8,128)(2,1)} copy(bf16[32,3584]{1,0:T(8,128)(2,1)} %get-tuple-element.4) | data formatting | bytes 458752
  114.3 1.3 %copy.20 = f32[28,128]{1,0:T(8,128)} copy(f32[28,128]{1,0:T(8,128)} %get-tuple-element.5) | data formatting | bytes 28672
